TPU v7x, 32 devices: a whole 2x2x4 slice. The times are simulated.
32 devices in a mesh: engine: 8 (over y, x, core), tensor: 4 (over z).
Axes of the slice: x: 2, y: 2, z: 4, core: 2. Of those that a mesh axis runs over, the one named last changes fastest.
Arguments:
- hidden: bfloat16 [4096, 5120], P('engine'), may hold values from -6 to 6
- lengths: int32 [16], replicated, may hold values from 1 to 256, as said below
- assignment: int32 [16], replicated, may hold values from 0 to 7, as said below
- wq: bfloat16 [2, 5120, 4096], P(None, ('engine', 'tensor')), may hold values from -0.078125 to 0.078125
- wkv: bfloat16 [2, 5120, 2048], P(None, ('engine', 'tensor')), may hold values from -0.078125 to 0.078125
- wo: bfloat16 [2, 4096, 5120], P(None, None, ('engine', 'tensor')), may hold values from -0.5 to 0.5
- norm_gain: float32 [2, 5120], replicated, may hold values from 0.5 to 1.5
- qk_gain: float32 [2, 2, 128], replicated, may hold values from 0.5 to 1.5
Outputs:
- new_hidden: bfloat16 [4096, 5120], P('engine')
- kv_cache: bfloat16 [2, 4096, 2048], P(None, 'engine', 'tensor')
Inputs may be any that keep to these rules, and one draw needn't show every extreme that they name: `lengths`: each rollout has 1 to 256 tokens; in every draw all rollouts of some engine have exactly 256. `assignment`: every engine is named by exactly 2 rollouts, so an engine's rollouts fill at most its 512 rows, and some engine's fill all of them.
All inputs are finite; a program needn't handle non-finite values.
Results may differ from a plain program's by a relative error of at most 0.018.
Values may be sent and summed in bfloat16 or wider, within the bound.
A program may use at most 128 MiB of HBM per device.

v0:
```python
import jax
import jax.numpy as jnp
from jax import lax
from jax.sharding import PartitionSpec as P

EPS = 1e-06
THETA = 1000000.0


def row_layout(lengths, assignment, engine, row_count):
    on_engine = assignment == engine
    own_sizes = jnp.where(on_engine, lengths, 0)
    offsets = jnp.cumsum(own_sizes) - own_sizes
    row_ids = jnp.arange(row_count, dtype=jnp.int32)
    inside = (
        on_engine[None, :]
        & (row_ids[:, None] >= offsets[None, :])
        & (row_ids[:, None] < (offsets + own_sizes)[None, :])
    )
    inside_int = inside.astype(jnp.int32)
    seq_index = jnp.arange(lengths.shape[0], dtype=jnp.int32)
    live_count = jnp.sum(inside_int, axis=1)
    segment = jnp.sum(inside_int * seq_index[None, :], axis=1)
    segment = jnp.where(live_count > 0, segment, lengths.shape[0] + row_ids)
    position = row_ids - jnp.sum(inside_int * offsets[None, :], axis=1)
    position = jnp.where(live_count > 0, position, 0)
    return (segment, position)


def rope_tables(position, head_size):
    half_width = head_size // 2
    frequency = jnp.power(
        jnp.float32(THETA), -(jnp.arange(half_width, dtype=jnp.float32) * 2.0 / head_size)
    )
    angles = position.astype(jnp.float32)[:, None] * frequency[None, :]
    return (jnp.cos(angles)[:, None, :], jnp.sin(angles)[:, None, :])


def rotate(values, cosine, sine_part):
    half_width = values.shape[-1] // 2
    first_half = values[..., :half_width]
    second_half = values[..., half_width:]
    return jnp.concatenate(
        [
            first_half * cosine - second_half * sine_part,
            second_half * cosine + first_half * sine_part,
        ],
        axis=-1,
    )


def head_norm(values, gain_row):
    return values * lax.rsqrt(jnp.mean(values * values, axis=-1, keepdims=True) + EPS) * gain_row


def norm_rows(values, gain_row):
    widened = values.astype(jnp.float32)
    return (
        widened * lax.rsqrt(jnp.mean(widened * widened, axis=-1, keepdims=True) + EPS) * gain_row
    ).astype(jnp.bfloat16)


def attend(queries, key_heads, value_heads, segment):
    row_count = queries.shape[0]
    scores = jnp.einsum(
        "rkgd,ckd->kgrc", queries, key_heads, preferred_element_type=jnp.float32
    ) * queries.shape[-1] ** (-0.5)
    row_ids = jnp.arange(row_count, dtype=jnp.int32)
    allowed = (segment[:, None] == segment[None, :]) & (row_ids[None, :] <= row_ids[:, None])
    raised = jnp.exp(scores) * allowed.astype(jnp.float32)
    weights = (raised / jnp.sum(raised, axis=-1, keepdims=True)).astype(jnp.bfloat16)
    attended = jnp.einsum(
        "kgrc,ckd->rkgd", weights, value_heads, preferred_element_type=jnp.float32
    )
    return attended.astype(jnp.bfloat16).reshape(row_count, -1)


def shards(hidden, lengths, assignment, wq, wkv, wo, norm_gain, qk_gain):
    row_count = hidden.shape[0]
    tensor_size = lax.axis_size("tensor")
    head_size = qk_gain.shape[-1]
    layer_total = wq.shape[0]
    local_queries = wq.shape[2] // tensor_size // head_size
    local_keys = wkv.shape[2] // tensor_size // (2 * head_size)
    segment, position = row_layout(lengths, assignment, lax.axis_index("engine"), row_count)
    cosine, sine_part = rope_tables(position, head_size)
    residual = hidden
    normed = norm_rows(hidden, norm_gain[0])
    caches = []
    for layer_number in range(layer_total):
        if layer_number > 0:
            normed = norm_rows(residual, norm_gain[layer_number])
        query_part, keyval_part = (
            lax.all_to_all(wq[layer_number], "tensor", split_axis=1, concat_axis=0, tiled=True),
            lax.all_to_all(wkv[layer_number], "tensor", split_axis=1, concat_axis=0, tiled=True),
        )
        query_weight, keyval_weight = (
            lax.all_gather(query_part, "engine", axis=0, tiled=True),
            lax.all_gather(keyval_part, "engine", axis=0, tiled=True),
        )
        queries = jnp.dot(normed, query_weight, preferred_element_type=jnp.float32)
        keyvals = jnp.dot(normed, keyval_weight, preferred_element_type=jnp.float32)
        queries = queries.reshape(row_count, local_queries, head_size)
        keyvals = keyvals.reshape(row_count, local_keys, 2, head_size)
        queries = rotate(head_norm(queries, qk_gain[layer_number, 0]), cosine, sine_part).astype(
            jnp.bfloat16
        )
        key_heads = rotate(
            head_norm(keyvals[:, :, 0], qk_gain[layer_number, 1]), cosine, sine_part
        ).astype(jnp.bfloat16)
        value_heads = keyvals[:, :, 1].astype(jnp.bfloat16)
        caches.append(
            jnp.stack([key_heads, value_heads], axis=2).reshape(
                row_count, local_keys * 2 * head_size
            )
        )
        attended = attend(
            queries.reshape(row_count, local_keys, local_queries // local_keys, head_size),
            key_heads,
            value_heads,
            segment,
        )
        out_part = lax.all_to_all(
            wo[layer_number], "tensor", split_axis=0, concat_axis=1, tiled=True
        )
        out_weight = lax.all_gather(out_part, "engine", axis=1, tiled=True)
        partial_term = jnp.dot(attended, out_weight, preferred_element_type=jnp.float32)
        summed = lax.psum(partial_term.astype(jnp.bfloat16), "tensor").astype(jnp.float32)
        residual = (residual.astype(jnp.float32) + summed).astype(jnp.bfloat16)
    return (residual, jnp.stack(caches))


def solution(mesh):
    return jax.shard_map(
        shards,
        mesh=mesh,
        in_specs=(
            P("engine", None),
            P(),
            P(),
            P(None, ("engine", "tensor"), None),
            P(None, ("engine", "tensor"), None),
            P(None, None, ("engine", "tensor")),
            P(),
            P(),
        ),
        out_specs=(P("engine", None), P(None, "engine", "tensor")),
        check_vma=False,
    )
```

profile of v0, /device:TPU:0, one launch (start us, length us, event | category | flops | bytes accessed | tf_op | source)
XLA Modules:
  0.0 857.2 jit_solution(12810951714542809549)
XLA Ops:
  7.2 2.2 fusion.51
  9.4 0.5 all_to_all.84
  10.1 23.5 %all_to_all.114 = bf16[160,4,512]{2,0,1:T(8,128)(2,1)} all-to-all(bf16[160,4,512]{2,0,1:T(8,128)(2,1)S(1)} %copy.127), channel_id=1, replica_groups=mesh['engine'=8,'tensor'=4] {'tensor'}, dimensions={1} | all-to-all | bytes 1310720 | tf_op jit(solution)/shard_map/all_to_all | solution.py:95
  33.6 3.0 fusion.50
  36.7 1.0 all_to_all.88
  37.7 0.4 copy.131
  38.1 33.7 %all_to_all.115 = bf16[160,4,1024]{2,0,1:T(8,128)(2,1)} all-to-all(bf16[160,4,1024]{2,0,1:T(8,128)(2,1)S(1)} %copy.131), channel_id=1, replica_groups=mesh['engine'=8,'tensor'=4] {'tensor'}, dimensions={1} | all-to-all | bytes 2621440 | tf_op jit(solution)/shard_map/all_to_all | solution.py:94
  71.8 3.1 fusion.49
  74.9 1.0 all_to_all.92
  75.9 0.4 copy.138
  76.3 33.6 %all_to_all.116 = bf16[4,1024,160]{1,2,0:T(8,128)(2,1)} all-to-all(bf16[4,1024,160]{1,2,0:T(8,128)(2,1)S(1)} %copy.138), channel_id=1, replica_groups=mesh['engine'=8,'tensor'=4] {'tensor'}, dimensions={0} | all-to-all | bytes 2621440 | tf_op jit(solution)/shard_map/all_to_all | solution.py:123
  110.4 3.6 fusion
  114.0 1.0 multiply_cosine_fusion
  115.3 7.8 fusion.16
  123.4 0.8 copy.163
  124.2 0.2 fusion.32
  124.7 1.0 subtract_convert_fusion.3
  125.7 13.5 %all-gather.9.cloned.1.call-done = bf16[5120,1024]{1,0:T(8,128)(2,1)} async-done(((bf16[640,1024]{1,0:T(8,128)(2,1)}), bf16[5120,1024]{1,0:T(8,128)(2,1)}) %all-gather.9.cloned.1.call-update) | async-done | bytes 10485776 | tf_op jit(solution)/shard_map/all_gather | solution.py:98
  139.2 9.9 %convolution_bitcast_fusion.1 = f32[64,8,8,128]{3,1,2,0:T(8,128)S(1)} fusion(bf16[5120,1024]{1,0:T(8,128)(2,1)} %all-gather.9.cloned.1.call-done, bf16[512,5120]{1,0:T(8,128)(2,1)} %param.8, f32[5120]{0:T(1024)S(1)} %bitcast.153, f32[512]{0:T(512)S(1)} %add_rsqrt_fusion.5), kind=kOutput, calls=%fused_computation.33 | convolution fusion | flops 5379194880 | bytes 17848320 | tf_op jit(solution)/shard_map/dot_general | solution.py:101
  149.1 0.5 copy.167
  149.6 1.3 multiply_reduce_fusion.1
  150.9 1.1 copy.132
  152.0 0.8 copy.133
  152.8 1.6 multiply_multiply_fusion.1
  154.4 1.9 subtract_convert_fusion.1
  156.6 2.4 fusion.8
  159.0 2.1 fusion.19
  161.2 43.2 %all-gather.11.cloned.1.call-done = bf16[1024,5120]{0,1:T(8,128)(2,1)} async-done(((bf16[1024,640]{0,1:T(8,128)(2,1)}), bf16[1024,5120]{0,1:T(8,128)(2,1)}) %all-gather.11.cloned.1.call-update) | async-done | bytes 10485776 | tf_op jit(solution)/shard_map/all_gather | solution.py:126
  204.3 11.7 %convolution_convert_fusion.1 = bf16[512,5120]{1,0:T(8,128)(2,1)} fusion(bf16[512,1024]{0,1:T(8,128)(2,1)S(1)} %bitcast.155, bf16[1024,5120]{0,1:T(8,128)(2,1)} %all-gather.11.cloned.1.call-done), kind=kOutput, calls=%fused_computation.19 | convolution fusion | flops 5371330560 | bytes 16777216 | tf_op jit(solution)/shard_map/dot_general | solution.py:127
  216.1 1.0 copy-done.5
  217.2 1.3 all_to_all.96
  218.5 1.2 copy.139
  219.7 37.8 %all_to_all.117 = bf16[160,4,512]{2,0,1:T(8,128)(2,1)} all-to-all(bf16[160,4,512]{2,0,1:T(8,128)(2,1)S(1)} %copy.139), channel_id=1, replica_groups=mesh['engine'=8,'tensor'=4] {'tensor'}, dimensions={1} | all-to-all | bytes 1310720 | tf_op jit(solution)/shard_map/all_to_all | solution.py:95
  257.6 1.9 all_to_all.100
  259.5 1.8 copy.142
  261.3 71.9 %all_to_all.118 = bf16[160,4,1024]{2,0,1:T(8,128)(2,1)} all-to-all(bf16[160,4,1024]{2,0,1:T(8,128)(2,1)S(1)} %copy.142), channel_id=1, replica_groups=mesh['engine'=8,'tensor'=4] {'tensor'}, dimensions={1} | all-to-all | bytes 2621440 | tf_op jit(solution)/shard_map/all_to_all | solution.py:94
  333.3 1.9 all_to_all.104
  335.2 1.7 copy.149
  336.9 42.4 %all_to_all.119 = bf16[4,1024,160]{1,2,0:T(8,128)(2,1)} all-to-all(bf16[4,1024,160]{1,2,0:T(8,128)(2,1)S(1)} %copy.149), channel_id=1, replica_groups=mesh['engine'=8,'tensor'=4] {'tensor'}, dimensions={0} | all-to-all | bytes 2621440 | tf_op jit(solution)/shard_map/all_to_all | solution.py:123
  379.3 91.0 %all-reduce.3.cloned.1.call-done = bf16[512,5120]{1,0:T(8,128)(2,1)} async-done(((bf16[512,5120]{1,0:T(8,128)(2,1)}), bf16[512,5120]{1,0:T(8,128)(2,1)}) %all-reduce.3.cloned.1.call-update) | async-done | bytes 5242896 | tf_op jit(solution)/shard_map/psum | solution.py:128
  470.3 8.8 %fusion.4 = (f32[512]{0:T(512)S(1)}, bf16[512,5120]{1,0:T(8,128)(2,1)}) fusion(bf16[512,5120]{1,0:T(8,128)(2,1)} %all-reduce.3.cloned.1.call-done, bf16[512,5120]{1,0:T(8,128)(2,1)} %param.8), kind=kLoop, calls=%fused_computation.10 | loop fusion | flops 18349568 | bytes 15730688 | tf_op jit(solution)/shard_map/reduce_sum | solution.py:59
  479.2 33.0 %all-gather.13.cloned.1.call-done = bf16[5120,512]{1,0:T(8,128)(2,1)} async-done(((bf16[640,512]{1,0:T(8,128)(2,1)}), bf16[5120,512]{1,0:T(8,128)(2,1)}) %all-gather.13.cloned.1.call-update) | async-done | bytes 5242896 | tf_op jit(solution)/shard_map/all_gather | solution.py:99
  512.2 7.8 fusion.13
  520.1 1.0 copy.166
  521.1 0.9 copy.165
  522.0 55.2 %all-gather.15.cloned.1.call-done = bf16[5120,1024]{1,0:T(8,128)(2,1)} async-done(((bf16[640,1024]{1,0:T(8,128)(2,1)}), bf16[5120,1024]{1,0:T(8,128)(2,1)}) %all-gather.15.cloned.1.call-update) | async-done | bytes 10485776 | tf_op jit(solution)/shard_map/all_gather | solution.py:98
  577.2 9.9 %convolution_bitcast_fusion = f32[64,8,8,128]{3,1,2,0:T(8,128)S(1)} fusion(bf16[5120,1024]{1,0:T(8,128)(2,1)} %all-gather.15.cloned.1.call-done, bf16[512,5120]{1,0:T(8,128)(2,1)} %get-tuple-element.18, f32[5120]{0:T(1024)S(1)} %bitcast.151, f32[512]{0:T(512)S(1)} %add_rsqrt_fusion.4), kind=kOutput, calls=%fused_computation.32 | convolution fusion | flops 5379194880 | bytes 17848320 | tf_op jit(solution)/shard_map/dot_general | solution.py:101
  587.1 0.5 copy.168
  587.6 1.3 multiply_reduce_fusion
  588.9 1.1 copy.143
  590.0 0.8 copy.144
  590.8 1.6 multiply_multiply_fusion
  592.5 1.9 subtract_convert_fusion
  594.7 0.2 fusion.30
  595.1 0.3 subtract_convert_fusion.2
  595.4 2.4 fusion.9
  597.8 2.9 fusion.18
  600.7 41.7 %all-gather.17.cloned.1.call-done = bf16[1024,5120]{0,1:T(8,128)(2,1)} async-done(((bf16[1024,640]{0,1:T(8,128)(2,1)}), bf16[1024,5120]{0,1:T(8,128)(2,1)}) %all-gather.17.cloned.1.call-update) | async-done | bytes 10485776 | tf_op jit(solution)/shard_map/all_gather | solution.py:126
  642.4 10.4 %convolution_convert_fusion = bf16[512,5120]{1,0:T(8,128)(2,1)} fusion(bf16[512,1024]{0,1:T(8,128)(2,1)} %bitcast.154, bf16[1024,5120]{0,1:T(8,128)(2,1)} %all-gather.17.cloned.1.call-done), kind=kOutput, calls=%fused_computation.18 | convolution fusion | flops 5371330560 | bytes 16777216 | tf_op jit(solution)/shard_map/dot_general | solution.py:127
  652.8 0.9 copy-done.7
  654.0 0.2 copy.150
  654.7 1.3 copy.152
  656.0 185.8 %all-reduce.5.cloned.1.call-done = bf16[512,5120]{1,0:T(8,128)(2,1)} async-done(((bf16[512,5120]{1,0:T(8,128)(2,1)}), bf16[512,5120]{1,0:T(8,128)(2,1)}) %all-reduce.5.cloned.1.call-update) | async-done | bytes 5242896 | tf_op jit(solution)/shard_map/psum | solution.py:128
  841.9 8.3 fusion.7
  (83 shorter events, 3.4 us)
Async XLA Ops:
  7.2 108.1 %all-gather.7.cloned.1.call-start = ((), (), s32[]{:S(2)}) async-start(), calls=%async_computation.6 | async-start | bytes 5898240 | tf_op jit(solution)/shard_map/all_gather | solution.py:99
  33.6 105.6 %all-gather.9.cloned.1.call-start = ((), (), s32[]{:S(2)}) async-start(), calls=%async_computation.7 | async-start | bytes 11796480 | tf_op jit(solution)/shard_map/all_gather | solution.py:98
  71.8 132.6 %all-gather.11.cloned.1.call-start = ((), (), s32[]{:S(2)}) async-start(), calls=%async_computation.8 | async-start | bytes 11796480 | tf_op jit(solution)/shard_map/all_gather | solution.py:126
  74.9 35.1 %copy-start.15 = (s32[16]{0:T(128)S(1)}, s32[16]{0:T(128)}, u32[]{:S(2)}) copy-start(s32[16]{0:T(128)} %param.9) | copy-start | bytes 196
  74.9 35.1 %copy-start.16 = (s32[16]{0:T(128)S(1)}, s32[16]{0:T(128)}, u32[]{:S(2)}) copy-start(s32[16]{0:T(128)} %param.10) | copy-start | bytes 196
  74.9 35.5 %copy-start.14 = (f32[2,2,128]{2,1,0:T(2,128)S(1)}, f32[2,2,128]{2,1,0:T(2,128)}, u32[]{:S(2)}) copy-start(f32[2,2,128]{2,1,0:T(2,128)} %param.15) | copy-start | bytes 6148
  76.3 38.9 %copy-start.13 = (f32[2,5120]{1,0:T(2,128)S(1)}, f32[2,5120]{1,0:T(2,128)}, u32[]{:S(2)}) copy-start(f32[2,5120]{1,0:T(2,128)} %param.14) | copy-start | bytes 122884
  109.9 360.4 %all-reduce.3.cloned.1.call-start = ((), (), s32[]{:S(2)}) async-start(), calls=%async_computation.9 | async-start | bytes 10485760 | tf_op jit(solution)/shard_map/psum | solution.py:128
  115.0 9.6 %copy-start = (f32[512,64]{1,0:T(8,128)}, f32[512,64]{1,0:T(8,128)S(1)}, u32[]{:S(2)}) copy-start(f32[512,64]{1,0:T(8,128)S(1)} %get-tuple-element.40) | copy-start | bytes 393220
  154.4 2.2 copy-start.6
  154.4 2.2 copy-start.8
  156.6 2.4 copy-start.10
  216.1 1.1 copy-start.5
  216.1 41.5 %copy-start.2 = (bf16[1,160,4096]{2,1,0:T(8,128)(2,1)S(1)}, bf16[1,160,4096]{2,1,0:T(8,128)(2,1)}, u32[]{:S(2)}) copy-start(bf16[1,160,4096]{2,1,0:T(8,128)(2,1)} %get-tuple-element.27) | copy-start | bytes 3932164
  216.1 296.1 %all-gather.13.cloned.1.call-start = ((), (), s32[]{:S(2)}) async-start(), calls=%async_computation.10 | async-start | bytes 5898240 | tf_op jit(solution)/shard_map/all_gather | solution.py:99
  257.5 319.7 %all-gather.15.cloned.1.call-start = ((), (), s32[]{:S(2)}) async-start(), calls=%async_computation.11 | async-start | bytes 11796480 | tf_op jit(solution)/shard_map/all_gather | solution.py:98
  259.5 73.8 %copy-start.3 = (bf16[1,4096,160]{1,2,0:T(8,128)(2,1)S(1)}, bf16[1,4096,160]{1,2,0:T(8,128)(2,1)}, u32[]{:S(2)}) copy-start(bf16[1,4096,160]{1,2,0:T(8,128)(2,1)} %get-tuple-element.23) | copy-start | bytes 3932164
  333.2 309.1 %all-gather.17.cloned.1.call-start = ((), (), s32[]{:S(2)}) async-start(), calls=%async_computation.12 | async-start | bytes 11796480 | tf_op jit(solution)/shard_map/all_gather | solution.py:126
  379.3 462.6 %all-reduce.5.cloned.1.call-start = ((), (), s32[]{:S(2)}) async-start(), calls=%async_computation.13 | async-start | bytes 10485760 | tf_op jit(solution)/shard_map/psum | solution.py:128
  592.4 2.2 copy-start.4
  592.5 2.7 copy-start.1
  595.4 2.4 copy-start.12
  652.7 0.9 copy-start.7
  652.7 1.0 copy-start.9
  652.7 1.1 copy-start.11
Sparse Core Ops, SparseCore 0:
  33.7 40.2 all-gather.6
  75.9 63.2 all-gather.8
  141.0 63.2 all-gather.10
  216.2 254.0 all-reduce.2
  472.0 40.0 all-gather.12
  513.9 63.2 all-gather.14
  579.1 63.2 all-gather.16
  652.9 188.9 all-reduce.4
where the time goes:
time: 863 us; the launch traced here: 857 us
  waiting for transfers between devices  464 us (54%)
  blocking collectives  243 us (28%)
  matrix products  67.3 us (8%)
  other arithmetic  34.4 us (4%)
  local copies, waits for them, and re-layouts  33.8 us (4%)
  between operations  14.9 us (2%)
    psum x2, waiting for transfers between devices, shards(): lax.psum(partial_term.astype(jnp.bfloat16), 'tensor').astype(jnp.float32)  277 us
    all_to_all x2, blocking collectives, shards(): lax.all_to_all(wq[layer_number], 'tensor', split_axis=1, concat_axis=0, t...  106 us
    all_gather x2, waiting for transfers between devices, shards(): out_weight = lax.all_gather(out_part, 'engine', axis=1, tiled=True)  84.9 us
    all_to_all x2, blocking collectives, shards(): lax.all_to_all(wo[layer_number], 'tensor', split_axis=0, concat_axis=1, t...  76 us
    all_gather x2, waiting for transfers between devices, shards(): lax.all_gather(query_part, 'engine', axis=0, tiled=True)  68.7 us
    all_to_all x2, blocking collectives, shards(): lax.all_to_all(wkv[layer_number], 'tensor', split_axis=1, concat_axis=0,...  61.3 us
    all_gather x2, waiting for transfers between devices, shards(): lax.all_gather(keyval_part, 'engine', axis=0, tiled=True)  33 us
    dot_general x2, matrix products, shards(): jnp.dot(attended, out_weight, preferred_element_type=jnp.float32)  22.1 us
  transfers between devices with their start and end apart: 8, of which 7 were waited for; matrix products, arithmetic and copies ran while one was open for 11% of the time, Pallas kernels for 0%

commit v1 on v0

--- a/solution.py
+++ b/solution.py
@@ -1,6 +1,10 @@
+import functools
+
 import jax
 import jax.numpy as jnp
 from jax import lax
+from jax.experimental import pallas as pl
+from jax.experimental.pallas import tpu as pltpu
 from jax.sharding import PartitionSpec as P
 
 EPS = 1e-06
@@ -130,9 +134,299 @@
     return (residual, jnp.stack(caches))
 
 
+MESH = pl.DeviceIdType.MESH
+ENGINES, TENSORS = 8, 4
+SUM_CHUNKS = 16
+
+
+def comm_kernel(n_gather, with_sum, *refs):
+    refs = list(refs)
+    ins = [refs.pop(0) for _ in range(n_gather)]
+    if with_sum:
+        term, resid = refs.pop(0), refs.pop(0)
+    outs = [refs.pop(0) for _ in range(n_gather)]
+    if with_sum:
+        total = refs.pop(0)
+    if n_gather:
+        own_sem, zs, zr, ps, pr, ds, dr, cs, cr = refs[:9]
+        refs = refs[9:]
+    if with_sum:
+        got_end, mine, got_mid, e_send, e_recv, m_send, m_recv, o_send, o_recv = refs
+
+    e, t = lax.axis_index("engine"), lax.axis_index("tensor")
+    core, xb, yb = e % 2, (e // 2) % 2, e // 4
+    sib, xn, yn = e + 1 - 2 * core, e + 2 - 4 * xb, e + 4 - 8 * yb
+    dg = xn + yn - e
+
+    barrier = pltpu.get_barrier_semaphore()
+    partners = [(e, (t + k) % TENSORS) for k in range(1, TENSORS)]
+    if n_gather:
+        partners += [(sib, t), (xn, t), (yn, t)]
+    for dev in partners:
+        pl.semaphore_signal(barrier, inc=1, device_id=dev, device_id_type=MESH)
+    pl.semaphore_wait(barrier, len(partners))
+
+    def rc(src, dst, ss, rs, dev):
+        return pltpu.make_async_remote_copy(
+            src_ref=src, dst_ref=dst, send_sem=ss, recv_sem=rs, device_id=dev, device_id_type=MESH
+        )
+
+    if n_gather:
+        rows = ins[0].shape[1]
+        half = rows // 2
+
+    def slot(k):
+        return (t + TENSORS - k) % TENSORS
+
+    def z_out(i, k):
+        to = (t + k) % TENSORS
+        return rc(ins[i].at[to], outs[i].at[e, t], zs.at[i, k - 1], zr.at[i, k - 1], (e, to))
+
+    def z_in(i, k):
+        here = outs[i].at[e, slot(k)]
+        return rc(here, here, zs.at[i, k - 1], zr.at[i, k - 1], (e, slot(k)))
+
+    def own(i):
+        return pltpu.make_async_copy(ins[i].at[t], outs[i].at[e, t], own_sem.at[i])
+
+    def plane(i, k, src, which):
+        there = outs[i].at[src, slot(k)]
+        source = ins[i].at[t] if k == 0 and src is e else there
+        dev = ((xn, t), (yn, t))[which]
+        return rc(source, there, ps.at[i, k, which], pr.at[i, k, which], dev)
+
+    def diag(i, k, src, which):
+        there = outs[i].at[src, slot(k), pl.ds(which * half, half)]
+        dev = ((yn, t), (xn, t))[which]
+        return rc(there, there, ds.at[i, k, which], dr.at[i, k, which], dev)
+
+    def cross(i, k, src, which):
+        there = outs[i].at[src, slot(k)]
+        source = ins[i].at[t] if k == 0 and which == 0 and src is e else there
+        return rc(source, there, cs.at[i, k, which], cr.at[i, k, which], (sib, t))
+
+    def stage0(i, k):
+        if k > 0:
+            z_in(i, k).wait_recv()
+        plane(i, k, e, 0).start()
+        plane(i, k, e, 1).start()
+        cross(i, k, e, 0).start()
+
+    def stage1(i, k):
+        plane(i, k, xn, 0).wait_recv()
+        diag(i, k, xn, 0).start()
+        cross(i, k, xn, 1).start()
+        plane(i, k, yn, 1).wait_recv()
+        diag(i, k, yn, 1).start()
+        cross(i, k, yn, 2).start()
+
+    def stage2(i, k):
+        diag(i, k, dg, 0).wait_recv()
+        diag(i, k, dg, 1).wait_recv()
+        cross(i, k, dg, 3).start()
+
+    def stage3(i, k):
+        sx, sy = xn + sib - e, yn + sib - e
+        for which, src in enumerate((sib, sx, sy, sx + sy - sib)):
+            cross(i, k, src, which).wait_recv()
+        if k > 0:
+            z_out(i, k).wait_send()
+        else:
+            own(i).wait()
+        plane(i, k, e, 0).wait_send()
+        plane(i, k, e, 1).wait_send()
+        diag(i, k, xn, 0).wait_send()
+        diag(i, k, yn, 1).wait_send()
+        for which, src in enumerate((e, xn, yn, dg)):
+            cross(i, k, src, which).wait_send()
+
+    is_end = (t == 0) | (t == TENSORS - 1)
+    end_peer = jnp.where(t < 2, 1 - t, 5 - t)
+    mid_peer = 3 - t
+
+    def band(ref, c):
+        size = ref.shape[0] // SUM_CHUNKS
+        return ref.at[pl.ds(c * size, size)]
+
+    def end_copy(c):
+        return rc(band(term, c), band(got_end, c), e_send.at[c], e_recv.at[c], (e, end_peer))
+
+    def mid_copy(c):
+        return rc(band(mine, c), band(got_mid, c), m_send.at[c], m_recv.at[c], (e, mid_peer))
+
+    def out_copy(c):
+        return rc(band(total, c), band(total, c), o_send.at[c], o_recv.at[c], (e, end_peer))
+
+    def sum_first(c):
+        @pl.when(jnp.logical_not(is_end))
+        def _():
+            end_copy(c).wait_recv()
+            band(mine, c)[...] = (
+                band(term, c)[...].astype(jnp.float32) + band(got_end, c)[...].astype(jnp.float32)
+            ).astype(jnp.bfloat16)
+            mid_copy(c).start()
+
+    def sum_second(c):
+        @pl.when(jnp.logical_not(is_end))
+        def _():
+            mid_copy(c).wait_recv()
+            both = band(mine, c)[...].astype(jnp.float32) + band(got_mid, c)[...].astype(jnp.float32)
+            band(total, c)[...] = (band(resid, c)[...].astype(jnp.float32) + both).astype(
+                jnp.bfloat16
+            )
+            out_copy(c).start()
+
+    if with_sum:
+
+        @pl.when(is_end)
+        def _():
+            @pl.loop(0, SUM_CHUNKS)
+            def _(c):
+                end_copy(c).start()
+
+    order = [(i, k) for i in range(n_gather) for k in range(TENSORS)]
+    for i in range(n_gather):
+        own(i).start()
+    for i in range(n_gather):
+        for k in range(1, TENSORS):
+            z_out(i, k).start()
+    steps = len(order) + 3 if n_gather else SUM_CHUNKS + 2
+    per_step = -(-(SUM_CHUNKS + 2) // max(1, len(order))) if n_gather else 1
+    done = 0
+    if with_sum and not n_gather:
+        sum_first(0)
+        sum_first(1)
+
+        @pl.loop(2, SUM_CHUNKS)
+        def _(c):
+            sum_first(c)
+            sum_second(c - 2)
+
+        sum_second(SUM_CHUNKS - 2)
+        sum_second(SUM_CHUNKS - 1)
+    if n_gather:
+        for step in range(steps):
+            if step < len(order):
+                stage0(*order[step])
+            if with_sum:
+                for _ in range(per_step):
+                    if done < SUM_CHUNKS:
+                        sum_first(done)
+                    if 2 <= done < SUM_CHUNKS + 2:
+                        sum_second(done - 2)
+                    done += 1
+            if 0 <= step - 1 < len(order):
+                stage1(*order[step - 1])
+            if 0 <= step - 2 < len(order):
+                stage2(*order[step - 2])
+        for item in order:
+            stage3(*item)
+    if with_sum:
+
+        @pl.when(is_end)
+        def _():
+            @pl.loop(0, SUM_CHUNKS)
+            def _(c):
+                out_copy(c).wait_recv()
+                end_copy(c).wait_send()
+
+        @pl.when(jnp.logical_not(is_end))
+        def _():
+            @pl.loop(0, SUM_CHUNKS)
+            def _(c):
+                mid_copy(c).wait_send()
+                out_copy(c).wait_send()
+
+
+def communicate(weights, sums, collective_id):
+    n = len(weights)
+    outs = [jax.ShapeDtypeStruct((ENGINES,) + w.shape, w.dtype) for w in weights]
+    in_specs = [pl.BlockSpec(memory_space=pl.ANY)] * n
+    out_specs = [pl.BlockSpec(memory_space=pl.ANY)] * n
+    scratch = []
+    dma = pltpu.SemaphoreType.DMA
+    if n:
+        scratch += [dma((n,)), dma((n, 3)), dma((n, 3))]
+        scratch += [dma((n, 4, 2))] * 4 + [dma((n, 4, 4))] * 2
+    if sums:
+        in_specs += [pl.BlockSpec(memory_space=pltpu.VMEM)] * 2
+        outs.append(jax.ShapeDtypeStruct(sums[0].shape, jnp.bfloat16))
+        out_specs.append(pl.BlockSpec(memory_space=pltpu.VMEM))
+        scratch += [pltpu.VMEM(sums[0].shape, jnp.bfloat16)] * 3
+        scratch += [dma((SUM_CHUNKS,))] * 6
+    return pl.pallas_call(
+        functools.partial(comm_kernel, n, bool(sums)),
+        out_shape=outs,
+        in_specs=in_specs,
+        out_specs=out_specs,
+        scratch_shapes=scratch,
+        compiler_params=pltpu.CompilerParams(
+            collective_id=collective_id, has_side_effects=True, vmem_limit_bytes=44 * 1024 * 1024
+        ),
+        cost_estimate=pl.CostEstimate(flops=0, bytes_accessed=60_000_000, transcendentals=0),
+    )(*weights, *sums)
+
+
+def fast_shards(hidden, lengths, assignment, wq, wkv, wo, norm_gain, qk_gain):
+    row_count, width = hidden.shape
+    head_size = qk_gain.shape[-1]
+    layer_total, depth = wq.shape[0], wq.shape[1]
+    q_width, kv_width = wq.shape[2] // TENSORS, wkv.shape[2] // TENSORS
+    local_queries, local_keys = q_width // head_size, kv_width // (2 * head_size)
+    segment, position = row_layout(lengths, assignment, lax.axis_index("engine"), row_count)
+    cosine, sine_part = rope_tables(position, head_size)
+
+    def by_target(layer_number):
+        queries = wq[layer_number].reshape(depth, TENSORS, q_width)
+        keyvals = wkv[layer_number].reshape(depth, TENSORS, kv_width)
+        both = jnp.concatenate([queries, keyvals], axis=2).transpose(1, 0, 2)
+        out = wo[layer_number].reshape(TENSORS, q_width, depth).transpose(0, 2, 1)
+        return [both, out]
+
+    residual = hidden
+    caches = []
+    weights = communicate(by_target(0), [], 1)
+    for layer_number in range(layer_total):
+        normed = norm_rows(residual, norm_gain[layer_number])
+        qkv_weight = weights[0].reshape(width, q_width + kv_width)
+        out_weight = weights[1].reshape(width, q_width)
+        projected = jnp.dot(normed, qkv_weight, preferred_element_type=jnp.float32)
+        queries = projected[:, :q_width].reshape(row_count, local_queries, head_size)
+        keyvals = projected[:, q_width:].reshape(row_count, local_keys, 2, head_size)
+        queries = rotate(head_norm(queries, qk_gain[layer_number, 0]), cosine, sine_part).astype(
+            jnp.bfloat16
+        )
+        key_heads = rotate(
+            head_norm(keyvals[:, :, 0], qk_gain[layer_number, 1]), cosine, sine_part
+        ).astype(jnp.bfloat16)
+        value_heads = keyvals[:, :, 1].astype(jnp.bfloat16)
+        caches.append(
+            jnp.stack([key_heads, value_heads], axis=2).reshape(
+                row_count, local_keys * 2 * head_size
+            )
+        )
+        attended = attend(
+            queries.reshape(row_count, local_keys, local_queries // local_keys, head_size),
+            key_heads,
+            value_heads,
+            segment,
+        )
+        term = lax.dot_general(
+            attended, out_weight, (((1,), (1,)), ((), ())), preferred_element_type=jnp.float32
+        ).astype(jnp.bfloat16)
+        if layer_number + 1 < layer_total:
+            *weights, residual = communicate(
+                by_target(layer_number + 1), [term, residual], 2 + layer_number
+            )
+        else:
+            (residual,) = communicate([], [term, residual], 2 + layer_number)
+    return (residual, jnp.stack(caches))
+
+
 def solution(mesh):
+    fits = mesh.shape["engine"] == ENGINES and mesh.shape["tensor"] == TENSORS
     return jax.shard_map(
-        shards,
+        fast_shards if fits else shards,
         mesh=mesh,
         in_specs=(
             P("engine", None),

time: 863 us -> 725 us (0.84)
  Pallas kernels: 0 us -> 582 us
  waiting for transfers between devices: 464 us -> 0 us
  blocking collectives: 243 us -> 0 us
  local copies, waits for them, and re-layouts: 33.8 us -> 50.5 us
  matrix products: 67.3 us -> 51.8 us
  between operations: 14.9 us -> 1.55 us
    pallas_call x0 -> x3, Pallas kernels: none -> 582 us  [communicate(): pl.pallas_call(functools.partial(comm_kernel, n, bool(sums)), out_shape=o...]
    psum x2 -> x0, waiting for transfers between devices: 277 us -> none  [shards(): lax.psum(partial_term.astype(jnp.bfloat16), 'tensor').astype(jnp.float32)]
    all_to_all x6 -> x0, blocking collectives: 243 us -> none  [the longest x2 106 us: shards(): lax.all_to_all(wq[layer_number], 'tensor', split_axis=1, concat_axis=0, t...]
    all_gather x6 -> x0, waiting for transfers between devices: 187 us -> none  [the longest x2 84.9 us: shards(): out_weight = lax.all_gather(out_part, 'engine', axis=1, tiled=True)]
    another operation x7 -> x19, local copies, waits for them, and re-layouts: 1.06 us -> 24.7 us  [the longest x4 10.6 us: by_target(): out = wo[layer_number].reshape(TENSORS, q_width, depth).transpose(0, 2, 1)]
    dot_general x6 -> x4, matrix products: 57.6 us -> 40.2 us  [the longest x2 25.2 us: fast_shards(): projected = jnp.dot(normed, qkv_weight, preferred_element_type=jnp.float32)]
    all_to_all x12 -> x0, local copies, waits for them, and re-layouts: 13.1 us -> none  [the longest x4 5.07 us: shards(): lax.all_to_all(wq[layer_number], 'tensor', split_axis=1, concat_axis=0, t...]
  transfers between devices with their start and end apart: 8 -> 0, of which waited for: 7 -> 0; matrix products, arithmetic and copies ran while one was open for 11% -> 0% of each run, Pallas kernels for 0% -> 0%
where the time goes in v1:
time: 725 us; the launch traced here: 715 us
  Pallas kernels  582 us (80%)
  matrix products  51.8 us (7%)
  local copies, waits for them, and re-layouts  50.5 us (7%)
  other arithmetic  28.9 us (4%)
    pallas_call x3, Pallas kernels, communicate(): pl.pallas_call(functools.partial(comm_kernel, n, bool(sums)), out_shape=o...  582 us
    dot_general x2, matrix products, fast_shards(): projected = jnp.dot(normed, qkv_weight, preferred_element_type=jnp.float32)  25.2 us
    dot_general x2, matrix products, fast_shards(): lax.dot_general(attended, out_weight, (((1,), (1,)), ((), ())), preferred...  15 us

profile of v1, /device:TPU:0, one launch (start us, length us, event | category | flops | bytes accessed | tf_op | source)
XLA Modules:
  0.0 715.3 jit_solution(8774918296966159907)
XLA Ops:
  0.7 0.8 fusion.41
  1.5 3.6 fusion
  5.1 0.6 slice_bitcast_fusion.3
  6.1 0.7 fusion.49
  6.7 1.8 multiply_cosine_fusion
  8.5 1.2 fusion.29
  9.8 0.5 reshape_squeeze.22
  10.4 0.5 reshape_squeeze.19
  10.9 1.0 copy.93
  11.8 1.9 fusion.47
  13.7 1.8 reshape_squeeze.21
  15.6 1.7 copy.95
  17.3 1.4 maximum_bitcast_fusion.1.refs_0_
  18.7 1.0 reshape_squeeze.18
  19.7 0.4 copy.92
  20.1 1.4 maximum_bitcast_fusion.refs_0_
  21.6 1.3 fusion.46
  22.9 1.8 reshape_squeeze.23
  24.8 1.7 copy.144
  26.5 4.1 reshape_squeeze.20
  30.6 2.9 copy.145
  33.5 123.6 %shard_map.95 = (bf16[8,4,160,1536]{3,2,1,0:T(8,128)(2,1)}, bf16[8,4,160,1024]{3,2,1,0:T(8,128)(2,1)}) custom-call(bf16[4,160,1536]{2,1,0:T(8,128)(2,1)S(1)} %copy-done.1, bf16[4,160,1024]{2,1,0:T(8,128)(2,1)S(1)} %bitcast.120), custom_call_target="tpu_custom_call" | custom-call | bytes 60000000 | tf_op jit(solution)/shard_map/pallas_call | solution.py:357
  157.2 13.2 %fusion.10 = f32[512,1536]{1,0:T(8,128)S(1)} fusion(bf16[5120,1536]{1,0:T(8,128)(2,1)} %bitcast.139, bf16[512,5120]{1,0:T(8,128)(2,1)} %refs_3_.1, f32[5120]{0:T(1024)S(1)} %bitcast.137, f32[512]{0:T(512)S(1)} %add_rsqrt_fusion.5), kind=kOutput, calls=%fused_computation.19 | convolution fusion | flops 8063549440 | bytes 24139776 | tf_op jit(solution)/shard_map/dot_general | solution.py:393
  170.4 1.1 slice.112
  171.6 1.8 copy.133
  173.4 1.9 reshape.308
  175.3 3.0 multiply_reduce_fusion.1
  178.3 1.0 copy.101
  179.3 0.6 add_rsqrt_fusion.1
  179.9 1.6 copy.102
  181.5 2.0 multiply_multiply_fusion.1
  183.5 1.9 subtract_convert_fusion.1
  185.4 1.2 copy.103
  186.5 0.4 slice.114
  186.9 0.5 slice.113
  188.3 0.7 copy-done.9
  189.0 1.0 pad_maximum_fusion.1
  190.0 2.0 copy.116
  192.0 1.4 copy.104
  193.4 3.9 fusion.6
  197.4 2.1 fusion.19
  199.6 0.7 slice-done.5
  200.2 7.5 %convolution_convert_fusion.1.refs_2_ = bf16[512,5120]{1,0:T(8,128)(2,1)} fusion(bf16[512,1024]{0,1:T(8,128)(2,1)S(1)} %bitcast.147, bf16[5120,1024]{1,0:T(8,128)(2,1)S(1)} %bitcast.145), kind=kOutput, calls=%fused_computation.15 | convolution fusion | flops 5371330560 | bytes 16777216 | tf_op jit(solution)/shard_map/dot_general | solution.py:414
  207.7 280.4 %shard_map.96 = (bf16[8,4,160,1536]{3,2,1,0:T(8,128)(2,1)}, bf16[8,4,160,1024]{3,2,1,0:T(8,128)(2,1)}, bf16[512,5120]{1,0:T(8,128)(2,1)S(1)}) custom-call(bf16[4,160,1536]{2,1,0:T(8,128)(2,1)S(1)} %maximum_bitcast_fusion.refs_0_, bf16[4,160,1024]{2,1,0:T(8,128)(2,1)S(1)} %bitcast.121, bf16[512,5120]{1,0:T(8,128)(2,1)} %convolution_convert_fusion.1.refs_2_, ...), custom_call_target="tpu_custom_call" | custom-call | bytes 60000000 | tf_op jit(solution)/shard_map/pallas_call | solution.py:357
  488.1 1.1 fusion.3
  489.3 11.9 %fusion.8 = f32[512,1536]{1,0:T(8,128)S(1)} fusion(bf16[5120,1536]{1,0:T(8,128)(2,1)} %bitcast.138, bf16[512,5120]{1,0:T(8,128)(2,1)S(1)} %get-tuple-element.9.refs_1_, f32[5120]{0:T(1024)S(1)} %bitcast.136, f32[512]{0:T(512)S(1)} %add_rsqrt_fusion.4), kind=kOutput, calls=%fused_computation.18 | convolution fusion | flops 8063549440 | bytes 24139776 | tf_op jit(solution)/shard_map/dot_general | solution.py:393
  501.5 1.8 copy.134
  503.3 1.3 copy.107
  504.6 1.1 slice.121
  505.6 1.1 slice.122
  506.9 0.8 copy.131
  508.5 2.4 multiply_reduce_fusion
  511.2 1.9 multiply_multiply_fusion
  513.1 1.9 subtract_convert_fusion
  515.3 1.0 copy.117
  516.3 1.3 pad_maximum_fusion
  517.6 1.3 copy.118
  519.0 1.4 copy.113
  520.3 3.5 fusion.7
  523.9 2.1 fusion.18
  526.0 0.7 slice-done.2
  526.7 7.5 %convolution_convert_fusion.refs_0_ = bf16[512,5120]{1,0:T(8,128)(2,1)} fusion(bf16[512,1024]{0,1:T(8,128)(2,1)S(1)} %bitcast.146, bf16[5120,1024]{1,0:T(8,128)(2,1)S(1)} %bitcast.142), kind=kOutput, calls=%fused_computation.14 | convolution fusion | flops 5371330560 | bytes 16777216 | tf_op jit(solution)/shard_map/dot_general | solution.py:414
  534.2 178.4 %shard_map.97 = bf16[512,5120]{1,0:T(8,128)(2,1)S(1)} custom-call(bf16[512,5120]{1,0:T(8,128)(2,1)} %convolution_convert_fusion.refs_0_, bf16[512,5120]{1,0:T(8,128)(2,1)} %copy-done), custom_call_target="tpu_custom_call" | custom-call | bytes 60000000 | tf_op jit(solution)/shard_map/pallas_call | solution.py:357
  712.7 2.4 copy.147
  (89 shorter events, 3.5 us)
Async XLA Ops:
  0.6 5.3 copy-start.23
  0.6 4.4 copy-start.22
  0.7 5.4 copy-start.16
  0.7 9.0 %copy-start.11 = (bf16[2,160,2048]{2,1,0:T(8,128)(2,1)S(1)}, bf16[2,160,2048]{2,1,0:T(8,128)(2,1)}, u32[]{:S(2)}) copy-start(bf16[2,160,2048]{2,1,0:T(8,128)(2,1)} %param.12) | copy-start | bytes 3932164
  19.7 1.9 copy-start.5
  30.6 2.9 copy-start.1
  30.6 126.5 %copy-start.18 = (f32[1,5120]{1,0:T(1,128)S(1)}, f32[1,5120]{1,0:T(1,128)}, u32[]{:S(2)}) copy-start(f32[1,5120]{1,0:T(1,128)} %get-tuple-element.42) | copy-start | bytes 61444
  175.3 8.2 %copy-start.4 = (f32[512,64]{1,0:T(8,128)S(1)}, f32[512,64]{1,0:T(8,128)}, u32[]{:S(2)}) copy-start(f32[512,64]{1,0:T(8,128)} %get-tuple-element.44) | copy-start | bytes 393220
  185.4 2.4 copy-start.21
  187.5 0.8 copy-start.12
  187.7 5.7 copy-start.3
  188.2 0.7 copy-start.9
  188.2 0.8 copy-start.10
  193.4 3.9 copy-start.13
  193.4 6.1 slice-start.3
  197.4 2.2 slice-start.4
  197.4 2.9 slice-start.5
  200.2 7.5 %copy-start.2 = (bf16[4,1024,160]{1,2,0:T(8,128)(2,1)S(1)}, bf16[4,1024,160]{1,2,0:T(8,128)(2,1)}, u32[]{:S(2)}) copy-start(bf16[4,1024,160]{1,2,0:T(8,128)(2,1)} %copy.145) | copy-start | bytes 3932164
  488.1 13.1 %copy-start = (bf16[512,5120]{1,0:T(8,128)(2,1)}, bf16[512,5120]{1,0:T(8,128)(2,1)S(1)}, u32[]{:S(2)}) copy-start(bf16[512,5120]{1,0:T(8,128)(2,1)S(1)} %get-tuple-element.9.refs_1_) | copy-start | bytes 15728644
  488.1 1.1 copy-start.17
  503.3 4.8 copy-start.20
  506.7 4.4 copy-start.19
  508.5 6.6 copy-start.6
  508.5 6.6 copy-start.8
  513.1 2.0 copy-start.14
  515.3 5.0 copy-start.7
  520.3 3.5 copy-start.15
  520.3 5.7 slice-start
  523.8 2.2 slice-start.1
  523.8 2.9 slice-start.2

commit v2 on v1

--- a/solution.py
+++ b/solution.py
@@ -136,20 +136,27 @@
 
 MESH = pl.DeviceIdType.MESH
 ENGINES, TENSORS = 8, 4
-SUM_CHUNKS = 16
-
-
-def comm_kernel(n_gather, with_sum, *refs):
+SUM_CHUNKS, WINDOW, LAG = 32, 6, 2
+
+
+def comm_kernel(parts, n_outs, with_sum, *refs):
     refs = list(refs)
-    ins = [refs.pop(0) for _ in range(n_gather)]
+    first = len(parts) > 0
+    n_in = len(parts) if first else n_outs
+    ins = [refs.pop(0) for _ in range(n_in)]
     if with_sum:
         term, resid = refs.pop(0), refs.pop(0)
-    outs = [refs.pop(0) for _ in range(n_gather)]
+    outs = [refs.pop(0) for _ in range(n_outs)]
+    if first:
+        staged = [refs.pop(0) for _ in range(n_outs)]
     if with_sum:
         total = refs.pop(0)
-    if n_gather:
-        own_sem, zs, zr, ps, pr, ds, dr, cs, cr = refs[:9]
-        refs = refs[9:]
+    if n_outs:
+        own_sem, ps, pr, ds, dr, cs, cr = refs[:7]
+        refs = refs[7:]
+    if first:
+        zs, zr = refs[:2]
+        refs = refs[2:]
     if with_sum:
         got_end, mine, got_mid, e_send, e_recv, m_send, m_recv, o_send, o_recv = refs
 
@@ -160,7 +167,7 @@
 
     barrier = pltpu.get_barrier_semaphore()
     partners = [(e, (t + k) % TENSORS) for k in range(1, TENSORS)]
-    if n_gather:
+    if n_outs:
         partners += [(sib, t), (xn, t), (yn, t)]
     for dev in partners:
         pl.semaphore_signal(barrier, inc=1, device_id=dev, device_id_type=MESH)
@@ -171,43 +178,64 @@
             src_ref=src, dst_ref=dst, send_sem=ss, recv_sem=rs, device_id=dev, device_id_type=MESH
         )
 
-    if n_gather:
-        rows = ins[0].shape[1]
-        half = rows // 2
-
     def slot(k):
         return (t + TENSORS - k) % TENSORS
 
-    def z_out(i, k):
+    def landing(layer, p, source):
+        out, column, size = parts[p]
+        ref = outs[out].at[e, source] if layer == 0 else staged[out].at[source]
+        return ref.at[:, pl.ds(column, size)]
+
+    def cut(layer, p, target):
+        size = parts[p][2]
+        return ins[p].at[layer, :, pl.ds(pl.multiple_of(target * size, 128), size)]
+
+    def z_out(layer, p, k):
         to = (t + k) % TENSORS
-        return rc(ins[i].at[to], outs[i].at[e, t], zs.at[i, k - 1], zr.at[i, k - 1], (e, to))
-
-    def z_in(i, k):
-        here = outs[i].at[e, slot(k)]
-        return rc(here, here, zs.at[i, k - 1], zr.at[i, k - 1], (e, slot(k)))
-
-    def own(i):
-        return pltpu.make_async_copy(ins[i].at[t], outs[i].at[e, t], own_sem.at[i])
+        sems = (zs.at[layer, p, k - 1], zr.at[layer, p, k - 1])
+        return rc(cut(layer, p, to), landing(layer, p, t), *sems, (e, to))
+
+    def z_in(layer, p, k):
+        here = landing(layer, p, slot(k))
+        return rc(here, here, zs.at[layer, p, k - 1], zr.at[layer, p, k - 1], (e, slot(k)))
+
+    def own(layer, p):
+        return pltpu.make_async_copy(
+            cut(layer, p, t), landing(layer, p, t), own_sem.at[layer, p]
+        )
+
+    def own_whole(i):
+        return pltpu.make_async_copy(ins[i], outs[i].at[e], own_sem.at[0, i])
+
+    def source_of(i, k):
+        return outs[i].at[e, slot(k)] if first else ins[i].at[slot(k)]
 
     def plane(i, k, src, which):
         there = outs[i].at[src, slot(k)]
-        source = ins[i].at[t] if k == 0 and src is e else there
         dev = ((xn, t), (yn, t))[which]
+        source = source_of(i, k) if src is e else there
         return rc(source, there, ps.at[i, k, which], pr.at[i, k, which], dev)
 
     def diag(i, k, src, which):
+        half = outs[i].shape[2] // 2
         there = outs[i].at[src, slot(k), pl.ds(which * half, half)]
         dev = ((yn, t), (xn, t))[which]
         return rc(there, there, ds.at[i, k, which], dr.at[i, k, which], dev)
 
     def cross(i, k, src, which):
         there = outs[i].at[src, slot(k)]
-        source = ins[i].at[t] if k == 0 and which == 0 and src is e else there
+        source = source_of(i, k) if src is e else there
         return rc(source, there, cs.at[i, k, which], cr.at[i, k, which], (sib, t))
 
+    def parts_of(i):
+        return [p for p in range(len(parts)) if parts[p][0] == i]
+
     def stage0(i, k):
-        if k > 0:
-            z_in(i, k).wait_recv()
+        for p in parts_of(i):
+            if k > 0:
+                z_in(0, p, k).wait_recv()
+            else:
+                own(0, p).wait()
         plane(i, k, e, 0).start()
         plane(i, k, e, 1).start()
         cross(i, k, e, 0).start()
@@ -229,10 +257,6 @@
         sx, sy = xn + sib - e, yn + sib - e
         for which, src in enumerate((sib, sx, sy, sx + sy - sib)):
             cross(i, k, src, which).wait_recv()
-        if k > 0:
-            z_out(i, k).wait_send()
-        else:
-            own(i).wait()
         plane(i, k, e, 0).wait_send()
         plane(i, k, e, 1).wait_send()
         diag(i, k, xn, 0).wait_send()
@@ -257,78 +281,106 @@
     def out_copy(c):
         return rc(band(total, c), band(total, c), o_send.at[c], o_recv.at[c], (e, end_peer))
 
-    def sum_first(c):
+    def wide(ref, c):
+        return band(ref, c)[...].astype(jnp.float32)
+
+    def mid_first(c):
+        end_copy(c).wait_recv()
+        band(mine, c)[...] = (wide(term, c) + wide(got_end, c)).astype(jnp.bfloat16)
+        mid_copy(c).start()
+
+    def mid_second(c):
+        mid_copy(c).wait_recv()
+        both = wide(mine, c) + wide(got_mid, c)
+        band(total, c)[...] = (wide(resid, c) + both).astype(jnp.bfloat16)
+        out_copy(c).start()
+
+    def sum_steps(low, high):
+        def each(start, stop, body):
+            start, stop = max(low, start), min(high, stop)
+            if start < stop:
+
+                @pl.loop(start, stop)
+                def _(c):
+                    body(c)
+
+        @pl.when(is_end)
+        def _():
+            each(0, WINDOW, lambda c: end_copy(c).start())
+
+            def later(c):
+                end_copy(c - WINDOW).wait_send()
+                end_copy(c).start()
+
+            each(WINDOW, SUM_CHUNKS, later)
+
         @pl.when(jnp.logical_not(is_end))
         def _():
-            end_copy(c).wait_recv()
-            band(mine, c)[...] = (
-                band(term, c)[...].astype(jnp.float32) + band(got_end, c)[...].astype(jnp.float32)
-            ).astype(jnp.bfloat16)
-            mid_copy(c).start()
-
-    def sum_second(c):
-        @pl.when(jnp.logical_not(is_end))
-        def _():
-            mid_copy(c).wait_recv()
-            both = band(mine, c)[...].astype(jnp.float32) + band(got_mid, c)[...].astype(jnp.float32)
-            band(total, c)[...] = (band(resid, c)[...].astype(jnp.float32) + both).astype(
-                jnp.bfloat16
-            )
-            out_copy(c).start()
-
-    if with_sum:
-
-        @pl.when(is_end)
-        def _():
-            @pl.loop(0, SUM_CHUNKS)
-            def _(c):
-                end_copy(c).start()
-
-    order = [(i, k) for i in range(n_gather) for k in range(TENSORS)]
-    for i in range(n_gather):
-        own(i).start()
-    for i in range(n_gather):
-        for k in range(1, TENSORS):
-            z_out(i, k).start()
-    steps = len(order) + 3 if n_gather else SUM_CHUNKS + 2
-    per_step = -(-(SUM_CHUNKS + 2) // max(1, len(order))) if n_gather else 1
-    done = 0
-    if with_sum and not n_gather:
-        sum_first(0)
-        sum_first(1)
-
-        @pl.loop(2, SUM_CHUNKS)
-        def _(c):
-            sum_first(c)
-            sum_second(c - 2)
-
-        sum_second(SUM_CHUNKS - 2)
-        sum_second(SUM_CHUNKS - 1)
-    if n_gather:
+            each(0, LAG, mid_first)
+
+            def both(c):
+                mid_first(c)
+                mid_second(c - LAG)
+
+            each(LAG, SUM_CHUNKS, both)
+            each(SUM_CHUNKS, SUM_CHUNKS + LAG, lambda c: mid_second(c - LAG))
+
+    order = [(i, k) for i in range(n_outs) for k in range(TENSORS)]
+    offsets = range(1, TENSORS)
+    z_plan = {}
+    if first:
+        for layer in range(2):
+            for p in range(len(parts)):
+                own(layer, p).start()
+        early = [(0, p, k) for k in offsets for p in parts_of(0)]
+        rest = [(layer, p, k) for layer in range(2) for i in range(n_outs) for k in offsets
+                for p in parts_of(i) if layer or i]
+        for item in early:
+            z_out(*item).start()
+        for n, item in enumerate(rest):
+            z_plan.setdefault(1 + n * (len(order) - 2) // len(rest), []).append(item)
+    elif n_outs:
+        for i in range(n_outs):
+            own_whole(i).start()
+    all_sums = SUM_CHUNKS + LAG
+    if with_sum and not n_outs:
+        sum_steps(0, all_sums)
+    if n_outs:
+        steps = len(order) + 2
         for step in range(steps):
             if step < len(order):
                 stage0(*order[step])
+                for item in z_plan.get(step, []):
+                    z_out(*item).start()
             if with_sum:
-                for _ in range(per_step):
-                    if done < SUM_CHUNKS:
-                        sum_first(done)
-                    if 2 <= done < SUM_CHUNKS + 2:
-                        sum_second(done - 2)
-                    done += 1
+                sum_steps(all_sums * step // steps, all_sums * (step + 1) // steps)
             if 0 <= step - 1 < len(order):
                 stage1(*order[step - 1])
             if 0 <= step - 2 < len(order):
                 stage2(*order[step - 2])
         for item in order:
             stage3(*item)
+    if first:
+        for p in range(len(parts)):
+            own(1, p).wait()
+            for k in offsets:
+                z_out(0, p, k).wait_send()
+                z_in(1, p, k).wait_recv()
+                z_out(1, p, k).wait_send()
+    elif n_outs:
+        for i in range(n_outs):
+            own_whole(i).wait()
     if with_sum:
 
         @pl.when(is_end)
         def _():
+            @pl.loop(SUM_CHUNKS - WINDOW, SUM_CHUNKS)
+            def _(c):
+                end_copy(c).wait_send()
+
             @pl.loop(0, SUM_CHUNKS)
             def _(c):
                 out_copy(c).wait_recv()
-                end_copy(c).wait_send()
 
         @pl.when(jnp.logical_not(is_end))
         def _():
@@ -338,16 +390,20 @@
                 out_copy(c).wait_send()
 
 
-def communicate(weights, sums, collective_id):
-    n = len(weights)
-    outs = [jax.ShapeDtypeStruct((ENGINES,) + w.shape, w.dtype) for w in weights]
-    in_specs = [pl.BlockSpec(memory_space=pl.ANY)] * n
-    out_specs = [pl.BlockSpec(memory_space=pl.ANY)] * n
+def communicate(sources, parts, blocks, sums, collective_id):
+    n = len(blocks)
+    dma = pltpu.SemaphoreType.DMA
+    outs = [jax.ShapeDtypeStruct((ENGINES, TENSORS) + b, jnp.bfloat16) for b in blocks]
+    if parts:
+        outs += [jax.ShapeDtypeStruct((TENSORS,) + b, jnp.bfloat16) for b in blocks]
+    in_specs = [pl.BlockSpec(memory_space=pl.ANY)] * len(sources)
+    out_specs = [pl.BlockSpec(memory_space=pl.ANY)] * len(outs)
     scratch = []
-    dma = pltpu.SemaphoreType.DMA
     if n:
-        scratch += [dma((n,)), dma((n, 3)), dma((n, 3))]
-        scratch += [dma((n, 4, 2))] * 4 + [dma((n, 4, 4))] * 2
+        scratch += [dma((2, max(n, len(parts))))] + [dma((n, TENSORS, 2))] * 4
+        scratch += [dma((n, TENSORS, 4))] * 2
+    if parts:
+        scratch += [dma((2, len(parts), TENSORS - 1))] * 2
     if sums:
         in_specs += [pl.BlockSpec(memory_space=pltpu.VMEM)] * 2
         outs.append(jax.ShapeDtypeStruct(sums[0].shape, jnp.bfloat16))
@@ -355,7 +411,7 @@
         scratch += [pltpu.VMEM(sums[0].shape, jnp.bfloat16)] * 3
         scratch += [dma((SUM_CHUNKS,))] * 6
     return pl.pallas_call(
-        functools.partial(comm_kernel, n, bool(sums)),
+        functools.partial(comm_kernel, parts, n, bool(sums)),
         out_shape=outs,
         in_specs=in_specs,
         out_specs=out_specs,
@@ -364,7 +420,61 @@
             collective_id=collective_id, has_side_effects=True, vmem_limit_bytes=44 * 1024 * 1024
         ),
         cost_estimate=pl.CostEstimate(flops=0, bytes_accessed=60_000_000, transcendentals=0),
-    )(*weights, *sums)
+    )(*sources, *sums)
+
+
+def attention_kernel(heads, keys, proj, cosine, sine_part, gain, allowed, attended, cache):
+    rows = proj.shape[0]
+    size = gain.shape[1]
+    block = rows // 2
+
+    def normed_rotated(low, high, column, which):
+        values = proj[low:high, column : column + size]
+        values = values * lax.rsqrt(jnp.mean(values * values, axis=-1, keepdims=True) + EPS)
+        values = values * gain[which : which + 1, :]
+        turned = values * cosine[low:high, :]
+        turned += pltpu.roll(values, size // 2, 1) * sine_part[low:high, :]
+        return turned.astype(jnp.bfloat16)
+
+    for key in range(keys):
+        column = heads * size + key * 2 * size
+        cache[:, key * 2 * size : key * 2 * size + size] = normed_rotated(0, rows, column, 1)
+        cache[:, key * 2 * size + size : (key + 1) * 2 * size] = proj[
+            :, column + size : column + 2 * size
+        ].astype(jnp.bfloat16)
+    for head in range(heads):
+        base = head // (heads // keys) * 2 * size
+        for low in range(0, rows, block):
+            high = low + block
+            queries = normed_rotated(low, high, head * size, 0)
+            scores = lax.dot_general(
+                queries,
+                cache[0:high, base : base + size],
+                (((1,), (1,)), ((), ())),
+                preferred_element_type=jnp.float32,
+            ) * size ** (-0.5)
+            raised = jnp.exp(scores) * allowed[low:high, 0:high]
+            share = 1.0 / jnp.sum(raised, axis=-1, keepdims=True)
+            weights = (raised * share).astype(jnp.bfloat16)
+            attended[low:high, head * size : (head + 1) * size] = jnp.dot(
+                weights,
+                cache[0:high, base + size : base + 2 * size],
+                preferred_element_type=jnp.float32,
+            ).astype(jnp.bfloat16)
+
+
+def attention(projected, cosine, sine_part, gain, allowed, heads, keys):
+    rows, size = projected.shape[0], gain.shape[-1]
+    return pl.pallas_call(
+        functools.partial(attention_kernel, heads, keys),
+        out_shape=[
+            jax.ShapeDtypeStruct((rows, heads * size), jnp.bfloat16),
+            jax.ShapeDtypeStruct((rows, keys * 2 * size), jnp.bfloat16),
+        ],
+        in_specs=[pl.BlockSpec(memory_space=pltpu.VMEM)] * 5,
+        out_specs=[pl.BlockSpec(memory_space=pltpu.VMEM)] * 2,
+        compiler_params=pltpu.CompilerParams(vmem_limit_bytes=40 * 1024 * 1024),
+    )(projected, cosine, sine_part, gain, allowed)
 
 
 def fast_shards(hidden, lengths, assignment, wq, wkv, wo, norm_gain, qk_gain):
@@ -372,54 +482,40 @@
     head_size = qk_gain.shape[-1]
     layer_total, depth = wq.shape[0], wq.shape[1]
     q_width, kv_width = wq.shape[2] // TENSORS, wkv.shape[2] // TENSORS
-    local_queries, local_keys = q_width // head_size, kv_width // (2 * head_size)
+    heads, keys = q_width // head_size, kv_width // (2 * head_size)
     segment, position = row_layout(lengths, assignment, lax.axis_index("engine"), row_count)
     cosine, sine_part = rope_tables(position, head_size)
-
-    def by_target(layer_number):
-        queries = wq[layer_number].reshape(depth, TENSORS, q_width)
-        keyvals = wkv[layer_number].reshape(depth, TENSORS, kv_width)
-        both = jnp.concatenate([queries, keyvals], axis=2).transpose(1, 0, 2)
-        out = wo[layer_number].reshape(TENSORS, q_width, depth).transpose(0, 2, 1)
-        return [both, out]
+    cosine = jnp.concatenate([cosine[:, 0], cosine[:, 0]], axis=1)
+    sine_part = jnp.concatenate([-sine_part[:, 0], sine_part[:, 0]], axis=1)
+    row_ids = jnp.arange(row_count, dtype=jnp.int32)
+    allowed = (segment[:, None] == segment[None, :]) & (row_ids[None, :] <= row_ids[:, None])
+    allowed = allowed.astype(jnp.float32)
 
     residual = hidden
     caches = []
-    weights = communicate(by_target(0), [], 1)
+    parts = ((0, 0, q_width), (0, q_width, kv_width), (1, 0, q_width))
+    blocks = [(depth, q_width + kv_width), (depth, q_width)]
+    *weights, staged_qkv, staged_out = communicate(
+        [wq, wkv, wo.transpose(0, 2, 1)], parts, blocks, [], 1
+    )
     for layer_number in range(layer_total):
         normed = norm_rows(residual, norm_gain[layer_number])
         qkv_weight = weights[0].reshape(width, q_width + kv_width)
         out_weight = weights[1].reshape(width, q_width)
         projected = jnp.dot(normed, qkv_weight, preferred_element_type=jnp.float32)
-        queries = projected[:, :q_width].reshape(row_count, local_queries, head_size)
-        keyvals = projected[:, q_width:].reshape(row_count, local_keys, 2, head_size)
-        queries = rotate(head_norm(queries, qk_gain[layer_number, 0]), cosine, sine_part).astype(
-            jnp.bfloat16
-        )
-        key_heads = rotate(
-            head_norm(keyvals[:, :, 0], qk_gain[layer_number, 1]), cosine, sine_part
-        ).astype(jnp.bfloat16)
-        value_heads = keyvals[:, :, 1].astype(jnp.bfloat16)
-        caches.append(
-            jnp.stack([key_heads, value_heads], axis=2).reshape(
-                row_count, local_keys * 2 * head_size
-            )
-        )
-        attended = attend(
-            queries.reshape(row_count, local_keys, local_queries // local_keys, head_size),
-            key_heads,
-            value_heads,
-            segment,
-        )
+        attended, cache = attention(
+            projected, cosine, sine_part, qk_gain[layer_number], allowed, heads, keys
+        )
+        caches.append(cache)
         term = lax.dot_general(
             attended, out_weight, (((1,), (1,)), ((), ())), preferred_element_type=jnp.float32
         ).astype(jnp.bfloat16)
         if layer_number + 1 < layer_total:
             *weights, residual = communicate(
-                by_target(layer_number + 1), [term, residual], 2 + layer_number
+                [staged_qkv, staged_out], (), blocks, [term, residual], 2
             )
         else:
-            (residual,) = communicate([], [term, residual], 2 + layer_number)
+            (residual,) = communicate([], (), [], [term, residual], 3)
     return (residual, jnp.stack(caches))
 
 

time: 725 us -> 497 us (0.69); the launches traced: 715 us -> 497 us
  Pallas kernels: 582 us -> 430 us
  local copies, waits for them, and re-layouts: 50.5 us -> 8.83 us
  other arithmetic: 28.9 us -> 8.76 us
    pallas_call x3 -> x5, Pallas kernels: 582 us -> 430 us  [the longest x3 415 us: communicate(): pl.pallas_call(functools.partial(comm_kernel, parts, n, bool(sums)), out_...]
    another operation x19 -> x1, local copies, waits for them, and re-layouts: 24.7 us -> 0.08 us  [the longest x4 10.6 us: by_target(): out = wo[layer_number].reshape(TENSORS, q_width, depth).transpose(0, 2, 1)]
    dot_general x4 -> x0, matrix products: 11.6 us -> none  [the longest x2 7.38 us: attend(): jnp.einsum('rkgd,ckd->kgrc', queries, key_heads, preferred_element_type=j...]
    slice x10 -> x0, local copies, waits for them, and re-layouts: 8.81 us -> none  [the longest x3 2.43 us: fast_shards(): projected[:, q_width:].reshape(row_count, local_keys, 2, head_size)]
    dot_general x2, matrix products: 15 us -> 23 us  [fast_shards(): lax.dot_general(attended, out_weight, (((1,), (1,)), ((), ())), preferred...]
where the time goes in v2:
time: 497 us
  Pallas kernels  430 us (87%)
  matrix products  47.9 us (10%)
  local copies, waits for them, and re-layouts  8.83 us (2%)
  other arithmetic  8.76 us (2%)
    pallas_call x3, Pallas kernels, communicate(): pl.pallas_call(functools.partial(comm_kernel, parts, n, bool(sums)), out_...  415 us
    dot_general x2, matrix products, fast_shards(): projected = jnp.dot(normed, qkv_weight, preferred_element_type=jnp.float32)  25 us
    dot_general x2, matrix products, fast_shards(): lax.dot_general(attended, out_weight, (((1,), (1,)), ((), ())), preferred...  23 us
    pallas_call x2, Pallas kernels, attention(): pl.pallas_call(functools.partial(attention_kernel, heads, keys), out_shap...  15.9 us

profile of v2, /device:TPU:0, one launch (start us, length us, event | category | flops | bytes accessed | tf_op | source)
XLA Modules:
  0.0 496.8 jit_solution(11228353892245031365)
XLA Ops:
  0.6 0.7 fusion.20
  1.3 3.6 fusion
  4.9 0.7 slice_bitcast_fusion
  5.6 0.1 copy.12
  5.7 0.1 reduce
  5.9 0.7 fusion.19
  6.5 0.1 select_reduce_fusion
  6.7 0.9 fusion.21
  7.6 1.0 fusion.16
  8.6 0.2 pad_maximum_fusion.1
  8.8 0.2 fusion.15.allowed
  8.9 0.0 copy-start.1
  9.0 1.7 copy-done.1
  10.7 0.0 copy-start.2
  10.7 1.7 copy-done.2
  12.4 0.0 copy-start.3
  12.4 1.3 copy-done.3
  13.7 142.2 %shard_map.95 = (bf16[8,4,160,1536]{3,2,1,0:T(8,128)(2,1)}, bf16[8,4,160,1024]{3,2,1,0:T(8,128)(2,1)}, bf16[4,160,1536]{2,1,0:T(8,128)(2,1)S(1)}, bf16[4,160,1024]{2,1,0:T(8,128)(2,1)S(1)}) custom-call(bf16[2,160,4096]{2,1,0:T(8,128)(2,1)S(1)} %copy-done.1, bf16[2,160,2048]{2,1,0:T(8,128)(2,1)S(1)} %copy-done.3, bf16[2,160,4096]{2,1,0:T(8,128)(2,1)S(1)} %bitcast.21), custom_call_target="tpu_custom_call" | custom-call | bytes 60000000 | tf_op jit(solution)/shard_map/pallas_call | solution.py:413
  156.0 12.9 %fusion.8.proj = f32[512,1536]{1,0:T(8,128)S(1)} fusion(bf16[5120,1536]{1,0:T(8,128)(2,1)} %bitcast.27, bf16[512,5120]{1,0:T(8,128)(2,1)} %refs_3_.1, f32[5120]{0:T(1024)S(1)} %bitcast.25, f32[512]{0:T(512)S(1)} %add_rsqrt_fusion.1), kind=kOutput, calls=%fused_computation.13 | convolution fusion | flops 8063549440 | bytes 24139776 | tf_op jit(solution)/shard_map/dot_general | solution.py:505
  168.9 8.0 %shard_map.96 = (bf16[512,1024]{1,0:T(8,128)(2,1)S(1)}, bf16[512,512]{1,0:T(8,128)(2,1)S(1)}) custom-call(f32[512,1536]{1,0:T(8,128)S(1)} %fusion.8.proj, f32[512,128]{1,0:T(8,128)S(1)} %get-tuple-element.38.cosine, f32[512,128]{1,0:T(8,128)S(1)} %get-tuple-element.39.sine_part, f32[2,128]{1,0:T(2,128)S(1)} %get-tuple-element.37.gain, ...), custom_call_target="tpu_custom_call" | custom-call | tf_op jit(solution)/shard_map/pallas_call | solution.py:468
  176.8 11.5 %convolution_convert_fusion.1.refs_2_ = bf16[512,5120]{1,0:T(8,128)(2,1)} fusion(bf16[512,1024]{1,0:T(8,128)(2,1)S(1)} %get-tuple-element.16, bf16[5120,1024]{1,0:T(8,128)(2,1)} %bitcast.29), kind=kOutput, calls=%fused_computation.11 | convolution fusion | flops 5371330560 | bytes 16777216 | tf_op jit(solution)/shard_map/dot_general | solution.py:510
  188.4 141.5 %shard_map.97 = (bf16[8,4,160,1536]{3,2,1,0:T(8,128)(2,1)}, bf16[8,4,160,1024]{3,2,1,0:T(8,128)(2,1)}, bf16[512,5120]{1,0:T(8,128)(2,1)S(1)}) custom-call(bf16[4,160,1536]{2,1,0:T(8,128)(2,1)S(1)} %get-tuple-element.13.refs_0_, bf16[4,160,1024]{2,1,0:T(8,128)(2,1)S(1)} %get-tuple-element.14.refs_1_, bf16[512,5120]{1,0:T(8,128)(2,1)} %convolution_convert_fusion.1.refs_2_, ...), custom_call_target="tpu_custom_call" | custom-call | bytes 60000000 | tf_op jit(solution)/shard_map/pallas_call | solution.py:413
  329.9 0.0 copy-start
  329.9 1.1 fusion.3
  331.0 12.1 %fusion.6.proj = f32[512,1536]{1,0:T(8,128)S(1)} fusion(bf16[5120,1536]{1,0:T(8,128)(2,1)} %bitcast.26, bf16[512,5120]{1,0:T(8,128)(2,1)S(1)} %get-tuple-element.18.refs_1_, f32[5120]{0:T(1024)S(1)} %bitcast.24, f32[512]{0:T(512)S(1)} %add_rsqrt_fusion), kind=kOutput, calls=%fused_computation.12 | convolution fusion | flops 8063549440 | bytes 24139776 | tf_op jit(solution)/shard_map/dot_general | solution.py:505
  343.1 0.0 copy-done
  343.1 8.0 %shard_map.98 = (bf16[512,1024]{1,0:T(8,128)(2,1)S(1)}, bf16[512,512]{1,0:T(8,128)(2,1)S(1)}) custom-call(f32[512,1536]{1,0:T(8,128)S(1)} %fusion.6.proj, f32[512,128]{1,0:T(8,128)S(1)} %get-tuple-element.38.cosine, f32[512,128]{1,0:T(8,128)S(1)} %get-tuple-element.39.sine_part, f32[2,128]{1,0:T(2,128)S(1)} %get-tuple-element.36.gain, ...), custom_call_target="tpu_custom_call" | custom-call | tf_op jit(solution)/shard_map/pallas_call | solution.py:468
  351.1 11.4 %convolution_convert_fusion.refs_0_ = bf16[512,5120]{1,0:T(8,128)(2,1)} fusion(bf16[512,1024]{1,0:T(8,128)(2,1)S(1)} %get-tuple-element.20, bf16[5120,1024]{1,0:T(8,128)(2,1)} %bitcast.28), kind=kOutput, calls=%fused_computation.10 | convolution fusion | flops 5371330560 | bytes 16777216 | tf_op jit(solution)/shard_map/dot_general | solution.py:510
  362.5 130.8 %shard_map.99 = bf16[512,5120]{1,0:T(8,128)(2,1)S(1)} custom-call(bf16[512,5120]{1,0:T(8,128)(2,1)} %convolution_convert_fusion.refs_0_, bf16[512,5120]{1,0:T(8,128)(2,1)} %copy-done), custom_call_target="tpu_custom_call" | custom-call | bytes 60000000 | tf_op jit(solution)/shard_map/pallas_call | solution.py:413
  493.4 1.1 pad_maximum_fusion
  494.4 2.4 copy.14
  (6 shorter events, 0.1 us)
Async XLA Ops:
  8.9 1.7 copy-start.1
  10.7 1.7 copy-start.2
  12.4 1.3 copy-start.3
  329.9 13.2 %copy-start = (bf16[512,5120]{1,0:T(8,128)(2,1)}, bf16[512,5120]{1,0:T(8,128)(2,1)S(1)}, u32[]{:S(2)}) copy-start(bf16[512,5120]{1,0:T(8,128)(2,1)S(1)} %get-tuple-element.18.refs_1_) | copy-start | bytes 15728644

commit v3 on v2

--- a/solution.py
+++ b/solution.py
@@ -136,19 +136,19 @@
 
 MESH = pl.DeviceIdType.MESH
 ENGINES, TENSORS = 8, 4
-SUM_CHUNKS, WINDOW, LAG = 32, 6, 2
+STRIP, WINDOW, LAG = 256, 4, 2
 
 
 def comm_kernel(parts, n_outs, with_sum, *refs):
     refs = list(refs)
     first = len(parts) > 0
-    n_in = len(parts) if first else n_outs
+    n_in = len(parts) if first else (1 + TENSORS if n_outs else 0)
     ins = [refs.pop(0) for _ in range(n_in)]
     if with_sum:
-        term, resid = refs.pop(0), refs.pop(0)
+        weight, left, resid = refs.pop(0), refs.pop(0), refs.pop(0)
     outs = [refs.pop(0) for _ in range(n_outs)]
     if first:
-        staged = [refs.pop(0) for _ in range(n_outs)]
+        staged = [refs.pop(0)]
     if with_sum:
         total = refs.pop(0)
     if n_outs:
@@ -158,7 +158,9 @@
         zs, zr = refs[:2]
         refs = refs[2:]
     if with_sum:
-        got_end, mine, got_mid, e_send, e_recv, m_send, m_recv, o_send, o_recv = refs
+        weight_in, term, got_end, got_mid = refs[:4]
+        w_sem, e_send, e_recv, m_send, m_recv, o_send, o_recv = refs[4:]
+        strips = term.shape[0]
 
     e, t = lax.axis_index("engine"), lax.axis_index("tensor")
     core, xb, yb = e % 2, (e // 2) % 2, e // 4
@@ -204,11 +206,13 @@
             cut(layer, p, t), landing(layer, p, t), own_sem.at[layer, p]
         )
 
-    def own_whole(i):
-        return pltpu.make_async_copy(ins[i], outs[i].at[e], own_sem.at[0, i])
-
     def source_of(i, k):
-        return outs[i].at[e, slot(k)] if first else ins[i].at[slot(k)]
+        if first:
+            return outs[i].at[e, slot(k)]
+        return ins[0].at[slot(k)] if i == 0 else ins[1 + k]
+
+    def own_later(i, k):
+        return pltpu.make_async_copy(source_of(i, k), outs[i].at[e, slot(k)], own_sem.at[i, k])
 
     def plane(i, k, src, which):
         there = outs[i].at[src, slot(k)]
@@ -268,31 +272,44 @@
     end_peer = jnp.where(t < 2, 1 - t, 5 - t)
     mid_peer = 3 - t
 
-    def band(ref, c):
-        size = ref.shape[0] // SUM_CHUNKS
-        return ref.at[pl.ds(c * size, size)]
+    def columns(ref, c):
+        return ref.at[:, pl.ds(pl.multiple_of(c * STRIP, STRIP), STRIP)]
+
+    def weight_copy(c):
+        return pltpu.make_async_copy(
+            weight.at[pl.ds(pl.multiple_of(c * STRIP, STRIP), STRIP)], weight_in.at[c], w_sem.at[c]
+        )
 
     def end_copy(c):
-        return rc(band(term, c), band(got_end, c), e_send.at[c], e_recv.at[c], (e, end_peer))
+        return rc(term.at[c], got_end.at[c], e_send.at[c], e_recv.at[c], (e, end_peer))
 
     def mid_copy(c):
-        return rc(band(mine, c), band(got_mid, c), m_send.at[c], m_recv.at[c], (e, mid_peer))
+        return rc(term.at[c], got_mid.at[c], m_send.at[c], m_recv.at[c], (e, mid_peer))
 
     def out_copy(c):
-        return rc(band(total, c), band(total, c), o_send.at[c], o_recv.at[c], (e, end_peer))
-
-    def wide(ref, c):
-        return band(ref, c)[...].astype(jnp.float32)
+        strip = columns(total, c)
+        return rc(strip, strip, o_send.at[c], o_recv.at[c], (e, end_peer))
+
+    def project(c):
+        weight_copy(c).wait()
+        term[c] = lax.dot_general(
+            left[...], weight_in[c], (((1,), (1,)), ((), ())), preferred_element_type=jnp.float32
+        ).astype(jnp.bfloat16)
 
     def mid_first(c):
+        project(c)
         end_copy(c).wait_recv()
-        band(mine, c)[...] = (wide(term, c) + wide(got_end, c)).astype(jnp.bfloat16)
+        term[c] = (term[c].astype(jnp.float32) + got_end[c].astype(jnp.float32)).astype(
+            jnp.bfloat16
+        )
         mid_copy(c).start()
 
     def mid_second(c):
         mid_copy(c).wait_recv()
-        both = wide(mine, c) + wide(got_mid, c)
-        band(total, c)[...] = (wide(resid, c) + both).astype(jnp.bfloat16)
+        both = term[c].astype(jnp.float32) + got_mid[c].astype(jnp.float32)
+        columns(total, c)[...] = (columns(resid, c)[...].astype(jnp.float32) + both).astype(
+            jnp.bfloat16
+        )
         out_copy(c).start()
 
     def sum_steps(low, high):
@@ -306,13 +323,18 @@
 
         @pl.when(is_end)
         def _():
-            each(0, WINDOW, lambda c: end_copy(c).start())
+            def early(c):
+                project(c)
+                end_copy(c).start()
+
+            each(0, WINDOW, early)
 
             def later(c):
+                project(c)
                 end_copy(c - WINDOW).wait_send()
                 end_copy(c).start()
 
-            each(WINDOW, SUM_CHUNKS, later)
+            each(WINDOW, strips, later)
 
         @pl.when(jnp.logical_not(is_end))
         def _():
@@ -322,8 +344,8 @@
                 mid_first(c)
                 mid_second(c - LAG)
 
-            each(LAG, SUM_CHUNKS, both)
-            each(SUM_CHUNKS, SUM_CHUNKS + LAG, lambda c: mid_second(c - LAG))
+            each(LAG, strips, both)
+            each(strips, strips + LAG, lambda c: mid_second(c - LAG))
 
     order = [(i, k) for i in range(n_outs) for k in range(TENSORS)]
     offsets = range(1, TENSORS)
@@ -331,18 +353,25 @@
     if first:
         for layer in range(2):
             for p in range(len(parts)):
-                own(layer, p).start()
+                if layer == 0 or parts[p][0] == 0:
+                    own(layer, p).start()
         early = [(0, p, k) for k in offsets for p in parts_of(0)]
-        rest = [(layer, p, k) for layer in range(2) for i in range(n_outs) for k in offsets
-                for p in parts_of(i) if layer or i]
+        rest = [(0, p, k) for k in offsets for p in parts_of(1)]
+        rest += [(1, p, k) for k in offsets for p in parts_of(0)]
         for item in early:
             z_out(*item).start()
         for n, item in enumerate(rest):
             z_plan.setdefault(1 + n * (len(order) - 2) // len(rest), []).append(item)
     elif n_outs:
-        for i in range(n_outs):
-            own_whole(i).start()
-    all_sums = SUM_CHUNKS + LAG
+        for item in order:
+            own_later(*item).start()
+    if with_sum:
+        all_sums = strips + LAG
+
+        @pl.loop(0, strips)
+        def _(c):
+            weight_copy(c).start()
+
     if with_sum and not n_outs:
         sum_steps(0, all_sums)
     if n_outs:
@@ -362,29 +391,31 @@
             stage3(*item)
     if first:
         for p in range(len(parts)):
+            for k in offsets:
+                z_out(0, p, k).wait_send()
+        for p in parts_of(0):
             own(1, p).wait()
             for k in offsets:
-                z_out(0, p, k).wait_send()
                 z_in(1, p, k).wait_recv()
                 z_out(1, p, k).wait_send()
     elif n_outs:
-        for i in range(n_outs):
-            own_whole(i).wait()
+        for item in order:
+            own_later(*item).wait()
     if with_sum:
 
         @pl.when(is_end)
         def _():
-            @pl.loop(SUM_CHUNKS - WINDOW, SUM_CHUNKS)
+            @pl.loop(strips - WINDOW, strips)
             def _(c):
                 end_copy(c).wait_send()
 
-            @pl.loop(0, SUM_CHUNKS)
+            @pl.loop(0, strips)
             def _(c):
                 out_copy(c).wait_recv()
 
         @pl.when(jnp.logical_not(is_end))
         def _():
-            @pl.loop(0, SUM_CHUNKS)
+            @pl.loop(0, strips)
             def _(c):
                 mid_copy(c).wait_send()
                 out_copy(c).wait_send()
@@ -395,21 +426,26 @@
     dma = pltpu.SemaphoreType.DMA
     outs = [jax.ShapeDtypeStruct((ENGINES, TENSORS) + b, jnp.bfloat16) for b in blocks]
     if parts:
-        outs += [jax.ShapeDtypeStruct((TENSORS,) + b, jnp.bfloat16) for b in blocks]
+        outs.append(jax.ShapeDtypeStruct((TENSORS,) + blocks[0], jnp.bfloat16))
     in_specs = [pl.BlockSpec(memory_space=pl.ANY)] * len(sources)
     out_specs = [pl.BlockSpec(memory_space=pl.ANY)] * len(outs)
     scratch = []
     if n:
-        scratch += [dma((2, max(n, len(parts))))] + [dma((n, TENSORS, 2))] * 4
+        scratch += [dma((2, TENSORS))] + [dma((n, TENSORS, 2))] * 4
         scratch += [dma((n, TENSORS, 4))] * 2
     if parts:
         scratch += [dma((2, len(parts), TENSORS - 1))] * 2
     if sums:
+        weight, left, resid = sums
+        rows, width = resid.shape
+        strips = width // STRIP
+        in_specs += [pl.BlockSpec(memory_space=pl.ANY)]
         in_specs += [pl.BlockSpec(memory_space=pltpu.VMEM)] * 2
-        outs.append(jax.ShapeDtypeStruct(sums[0].shape, jnp.bfloat16))
+        outs.append(jax.ShapeDtypeStruct(resid.shape, jnp.bfloat16))
         out_specs.append(pl.BlockSpec(memory_space=pltpu.VMEM))
-        scratch += [pltpu.VMEM(sums[0].shape, jnp.bfloat16)] * 3
-        scratch += [dma((SUM_CHUNKS,))] * 6
+        scratch += [pltpu.VMEM((strips, STRIP, left.shape[1]), jnp.bfloat16)]
+        scratch += [pltpu.VMEM((strips, rows, STRIP), jnp.bfloat16)] * 3
+        scratch += [dma((strips,))] * 7
     return pl.pallas_call(
         functools.partial(comm_kernel, parts, n, bool(sums)),
         out_shape=outs,
@@ -417,7 +453,7 @@
         out_specs=out_specs,
         scratch_shapes=scratch,
         compiler_params=pltpu.CompilerParams(
-            collective_id=collective_id, has_side_effects=True, vmem_limit_bytes=44 * 1024 * 1024
+            collective_id=collective_id, has_side_effects=True, vmem_limit_bytes=50 * 1024 * 1024
         ),
         cost_estimate=pl.CostEstimate(flops=0, bytes_accessed=60_000_000, transcendentals=0),
     )(*sources, *sums)
@@ -474,6 +510,11 @@
         in_specs=[pl.BlockSpec(memory_space=pltpu.VMEM)] * 5,
         out_specs=[pl.BlockSpec(memory_space=pltpu.VMEM)] * 2,
         compiler_params=pltpu.CompilerParams(vmem_limit_bytes=40 * 1024 * 1024),
+        cost_estimate=pl.CostEstimate(
+            flops=4 * heads * rows * rows * size,
+            bytes_accessed=projected.size * 8,
+            transcendentals=heads * rows * rows,
+        ),
     )(projected, cosine, sine_part, gain, allowed)
 
 
@@ -495,9 +536,17 @@
     caches = []
     parts = ((0, 0, q_width), (0, q_width, kv_width), (1, 0, q_width))
     blocks = [(depth, q_width + kv_width), (depth, q_width)]
-    *weights, staged_qkv, staged_out = communicate(
-        [wq, wkv, wo.transpose(0, 2, 1)], parts, blocks, [], 1
-    )
+    turned = wo.transpose(0, 2, 1)
+    *weights, staged = communicate([wq, wkv, turned], parts, blocks, [], 1)
+    staged, last = lax.optimization_barrier((staged, turned[1]))
+    place = lax.axis_index("tensor")
+    sources = [staged]
+    for k in range(TENSORS):
+        begin = (place + k) % TENSORS * q_width
+        piece = lax.dynamic_slice(last, (0, begin), (depth, q_width))
+        if k > 0:
+            piece = lax.ppermute(piece, "tensor", [(i, (i + k) % TENSORS) for i in range(TENSORS)])
+        sources.append(piece)
     for layer_number in range(layer_total):
         normed = norm_rows(residual, norm_gain[layer_number])
         qkv_weight = weights[0].reshape(width, q_width + kv_width)
@@ -507,15 +556,11 @@
             projected, cosine, sine_part, qk_gain[layer_number], allowed, heads, keys
         )
         caches.append(cache)
-        term = lax.dot_general(
-            attended, out_weight, (((1,), (1,)), ((), ())), preferred_element_type=jnp.float32
-        ).astype(jnp.bfloat16)
+        sums = [out_weight, attended, residual]
         if layer_number + 1 < layer_total:
-            *weights, residual = communicate(
-                [staged_qkv, staged_out], (), blocks, [term, residual], 2
-            )
+            *weights, residual = communicate(sources, (), blocks, sums, 2)
         else:
-            (residual,) = communicate([], (), [], [term, residual], 3)
+            (residual,) = communicate([], (), [], sums, 3)
     return (residual, jnp.stack(caches))
 
 

time: 497 us -> 497 us (level)
  matrix products: 47.9 us -> 24.3 us
  starting transfers between devices: 0 us -> 21.1 us
    dot_general x2 -> x0, matrix products: 23 us -> none  [fast_shards(): lax.dot_general(attended, out_weight, (((1,), (1,)), ((), ())), preferred...]
    ppermute x0 -> x3, starting transfers between devices: none -> 21.1 us  [fast_shards(): lax.ppermute(piece, 'tensor', [(i, (i + k) % TENSORS) for i in range(TENS...]
  transfers between devices with their start and end apart: 0 -> 3, of which waited for: 0 -> 0; matrix products, arithmetic and copies ran while one was open for 0% -> 4% of each run, Pallas kernels for 0% -> 2%
where the time goes in v3:
time: 497 us; the launch traced here: 496 us
  Pallas kernels  430 us (87%)
  matrix products  24.3 us (5%)
  starting transfers between devices  21.1 us (4%)
  other arithmetic  10.1 us (2%)
  local copies, waits for them, and re-layouts  9.7 us (2%)
    pallas_call x3, Pallas kernels, communicate(): pl.pallas_call(functools.partial(comm_kernel, parts, n, bool(sums)), out_...  414 us
    dot_general x2, matrix products, fast_shards(): projected = jnp.dot(normed, qkv_weight, preferred_element_type=jnp.float32)  24.3 us
    ppermute x3, starting transfers between devices, fast_shards(): lax.ppermute(piece, 'tensor', [(i, (i + k) % TENSORS) for i in range(TENS...  21.1 us
    pallas_call x2, Pallas kernels, attention(): pl.pallas_call(functools.partial(attention_kernel, heads, keys), out_shap...  15.9 us
  transfers between devices with their start and end apart: 3, of which 0 were waited for; matrix products, arithmetic and copies ran while one was open for 4% of the time, Pallas kernels for 2%

profile of v3, /device:TPU:0, one launch (start us, length us, event | category | flops | bytes accessed | tf_op | source)
XLA Modules:
  0.0 496.2 jit_solution(12057564347089508924)
XLA Ops:
  0.7 1.4 slice_bitcast_fusion
  2.1 0.0 copy-start.1
  2.1 1.3 copy-done.1
  3.4 128.4 %shard_map.95 = (bf16[8,4,160,1536]{3,2,1,0:T(8,128)(2,1)}, bf16[8,4,160,1024]{3,2,1,0:T(8,128)(2,1)}, bf16[4,160,1536]{2,1,0:T(8,128)(2,1)S(1)}) custom-call(bf16[2,160,4096]{2,1,0:T(8,128)(2,1)} %refs_0_.1, bf16[2,160,2048]{2,1,0:T(8,128)(2,1)S(1)} %copy-done.1, bf16[2,160,4096]{2,1,0:T(8,128)(2,1)} %bitcast.24), custom_call_target="tpu_custom_call" | custom-call | bytes 60000000 | tf_op jit(solution)/shard_map/pallas_call | solution.py:449
  131.9 0.0 copy-start
  131.9 1.3 copy-done
  133.1 0.0 copy-start.5
  133.1 0.0 copy-start.6
  133.1 0.0 copy-start.3
  133.1 0.1 constant_dynamic-slice_fusion
  133.3 20.5 %collective-permute-start.2 = (bf16[160,1024]{1,0:T(8,128)(2,1)S(1)}, bf16[160,1024]{1,0:T(8,128)(2,1)S(1)}, u32[]{:S(2)}, u32[]{:S(2)}) collective-permute-start(bf16[160,1024]{1,0:T(8,128)(2,1)S(1)} %get-tuple-element.33), channel_id=1, source_target_pairs={{0,3},{1,0},{2,1},{3,2},{4,7},{5,4},{6,5},{7,6},{8,11},{9,8},{10,9... | collective-permute-start | bytes 983048 | tf_op jit(solution)/shard_map/ppermute | solution.py:548
  153.7 0.0 collective-permute-start.1
  153.7 0.6 collective-permute-start
  154.4 3.6 fusion
  158.0 0.0 copy-done.5
  158.0 0.0 copy-done.6
  158.0 0.1 copy.12
  158.2 0.1 reduce
  158.3 0.1 select_reduce_fusion
  158.4 0.0 copy-done.3
  158.4 0.2 fusion.15.allowed
  158.6 1.0 fusion.16
  159.6 0.0 copy-start.4
  159.6 12.9 %fusion.8.proj = f32[512,1536]{1,0:T(8,128)S(1)} fusion(bf16[5120,1536]{1,0:T(8,128)(2,1)} %bitcast.27, bf16[512,5120]{1,0:T(8,128)(2,1)} %refs_7_.1, f32[5120]{0:T(1024)S(1)} %bitcast.26, f32[512]{0:T(512)S(1)} %add_rsqrt_fusion.1), kind=kOutput, calls=%fused_computation.11 | convolution fusion | flops 8063549440 | bytes 24139776 | tf_op jit(solution)/shard_map/dot_general | solution.py:554
  172.5 0.2 pad_maximum_fusion.1
  172.7 0.0 copy-done.4
  172.8 8.0 %shard_map.96 = (bf16[512,1024]{1,0:T(8,128)(2,1)S(1)}, bf16[512,512]{1,0:T(8,128)(2,1)S(1)}) custom-call(f32[512,1536]{1,0:T(8,128)S(1)} %fusion.8.proj, f32[512,128]{1,0:T(8,128)S(1)} %get-tuple-element.44.cosine, f32[512,128]{1,0:T(8,128)S(1)} %get-tuple-element.45.sine_part, f32[2,128]{1,0:T(2,128)S(1)} %get-tuple-element.43.gain, ...), custom_call_target="tpu_custom_call" | custom-call | flops 1073741824 | bytes 6291456 | tf_op jit(solution)/shard_map/pallas_call | solution.py:504
  180.7 0.0 collective-permute-done.2.refs_4_
  180.8 0.0 collective-permute-done.1.refs_3_
  180.8 0.0 collective-permute-done.refs_2_
  180.8 144.9 %shard_map.97 = (bf16[8,4,160,1536]{3,2,1,0:T(8,128)(2,1)}, bf16[8,4,160,1024]{3,2,1,0:T(8,128)(2,1)}, bf16[512,5120]{1,0:T(8,128)(2,1)}) custom-call(bf16[4,160,1536]{2,1,0:T(8,128)(2,1)} %copy-done, bf16[160,1024]{1,0:T(8,128)(2,1)S(1)} %get-tuple-element.36.refs_1_, bf16[160,1024]{1,0:T(8,128)(2,1)S(1)} %collective-permute-done.refs_2_, ...), custom_call_target="tpu_custom_call" | custom-call | bytes 60000000 | tf_op jit(solution)/shard_map/pallas_call | solution.py:449
  325.7 0.0 copy-start.2
  325.7 3.7 fusion.3
  329.5 0.3 copy-done.2
  329.8 11.4 %fusion.6.proj = f32[512,1536]{1,0:T(8,128)S(1)} fusion(bf16[5120,1536]{1,0:T(8,128)(2,1)} %bitcast.28, bf16[512,5120]{1,0:T(8,128)(2,1)S(1)} %copy-done.2, f32[5120]{0:T(1024)S(1)} %bitcast.25, f32[512]{0:T(512)S(1)} %add_rsqrt_fusion), kind=kOutput, calls=%fused_computation.10 | convolution fusion | flops 8063549440 | bytes 24139776 | tf_op jit(solution)/shard_map/dot_general | solution.py:554
  341.2 8.0 %shard_map.98 = (bf16[512,1024]{1,0:T(8,128)(2,1)S(1)}, bf16[512,512]{1,0:T(8,128)(2,1)S(1)}) custom-call(f32[512,1536]{1,0:T(8,128)S(1)} %fusion.6.proj, f32[512,128]{1,0:T(8,128)S(1)} %get-tuple-element.44.cosine, f32[512,128]{1,0:T(8,128)S(1)} %get-tuple-element.45.sine_part, f32[2,128]{1,0:T(2,128)S(1)} %get-tuple-element.42.gain, ...), custom_call_target="tpu_custom_call" | custom-call | flops 1073741824 | bytes 6291456 | tf_op jit(solution)/shard_map/pallas_call | solution.py:504
  349.2 140.8 %shard_map.99 = bf16[512,5120]{1,0:T(8,128)(2,1)} custom-call(bf16[5120,1024]{1,0:T(8,128)(2,1)} %bitcast.22, bf16[512,1024]{1,0:T(8,128)(2,1)S(1)} %get-tuple-element.23.refs_1_, bf16[512,5120]{1,0:T(8,128)(2,1)} %get-tuple-element.21.refs_2_), custom_call_target="tpu_custom_call" | custom-call | bytes 60000000 | tf_op jit(solution)/shard_map/pallas_call | solution.py:449
  490.0 1.1 pad_maximum_fusion
  491.0 5.2 %copy.14 = bf16[512,5120]{1,0:T(8,128)(2,1)} copy(bf16[512,5120]{1,0:T(8,128)(2,1)} %shard_map.99) | data formatting | bytes 10485760
  (10 shorter events, 0.1 us)
Async XLA Ops:
  2.1 1.3 copy-start.1
  131.9 1.3 copy-start
  133.1 24.9 %copy-start.5 = (s32[16]{0:T(128)S(1)}, s32[16]{0:T(128)}, u32[]{:S(2)}) copy-start(s32[16]{0:T(128)} %param.9) | copy-start | bytes 196
  133.1 24.9 %copy-start.6 = (s32[16]{0:T(128)S(1)}, s32[16]{0:T(128)}, u32[]{:S(2)}) copy-start(s32[16]{0:T(128)} %param.10) | copy-start | bytes 196
  133.1 25.2 %copy-start.3 = (f32[2,5120]{1,0:T(2,128)S(1)}, f32[2,5120]{1,0:T(2,128)}, u32[]{:S(2)}) copy-start(f32[2,5120]{1,0:T(2,128)} %param.14) | copy-start | bytes 122884
  133.3 47.5 %collective-permute-start.2 = (bf16[160,1024]{1,0:T(8,128)(2,1)S(1)}, bf16[160,1024]{1,0:T(8,128)(2,1)S(1)}, u32[]{:S(2)}, u32[]{:S(2)}) collective-permute-start(bf16[160,1024]{1,0:T(8,128)(2,1)S(1)} %get-tuple-element.33), channel_id=1, source_target_pairs={{0,3},{1,0},{2,1},{3,2},{4,7},{5,4},{6,5},{7,6},{8,11},{9,8},{10,9... | collective-permute-start | bytes 983048 | tf_op jit(solution)/shard_map/ppermute | solution.py:548
  153.7 27.0 %collective-permute-start.1 = (bf16[160,1024]{1,0:T(8,128)(2,1)S(1)}, bf16[160,1024]{1,0:T(8,128)(2,1)S(1)}, u32[]{:S(2)}, u32[]{:S(2)}) collective-permute-start(bf16[160,1024]{1,0:T(8,128)(2,1)S(1)} %get-tuple-element.34), channel_id=1, source_target_pairs={{0,2},{1,3},{2,0},{3,1},{4,6},{5,7},{6,4},{7,5},{8,10},{9,11},{10,... | collective-permute-start | bytes 983048 | tf_op jit(solution)/shard_map/ppermute | solution.py:548
  153.7 27.0 %collective-permute-start = (bf16[160,1024]{1,0:T(8,128)(2,1)S(1)}, bf16[160,1024]{1,0:T(8,128)(2,1)S(1)}, u32[]{:S(2)}, u32[]{:S(2)}) collective-permute-start(bf16[160,1024]{1,0:T(8,128)(2,1)S(1)} %get-tuple-element.35), channel_id=1, source_target_pairs={{0,1},{1,2},{2,3},{3,0},{4,5},{5,6},{6,7},{7,4},{8,9},{9,10},{10,1... | collective-permute-start | bytes 983048 | tf_op jit(solution)/shard_map/ppermute | solution.py:548
  159.6 13.1 %copy-start.4 = (f32[2,2,128]{2,1,0:T(2,128)S(1)}, f32[2,2,128]{2,1,0:T(2,128)}, u32[]{:S(2)}) copy-start(f32[2,2,128]{2,1,0:T(2,128)} %param.15) | copy-start | bytes 6148
  325.7 4.0 copy-start.2

commit v4 on v3

--- a/solution.py
+++ b/solution.py
@@ -136,7 +136,11 @@
 
 MESH = pl.DeviceIdType.MESH
 ENGINES, TENSORS = 8, 4
-STRIP, WINDOW, LAG = 256, 4, 2
+STRIP, WINDOW, LAG = 128, 4, 1
+
+
+def partner(place, k):
+    return (place, place + 1 - 2 * (place % 2), (place + 2) % 4, 3 - place)[k]
 
 
 def comm_kernel(parts, n_outs, with_sum, *refs):
@@ -181,7 +185,7 @@
         )
 
     def slot(k):
-        return (t + TENSORS - k) % TENSORS
+        return partner(t, k)
 
     def landing(layer, p, source):
         out, column, size = parts[p]
@@ -193,7 +197,7 @@
         return ins[p].at[layer, :, pl.ds(pl.multiple_of(target * size, 128), size)]
 
     def z_out(layer, p, k):
-        to = (t + k) % TENSORS
+        to = partner(t, k)
         sems = (zs.at[layer, p, k - 1], zr.at[layer, p, k - 1])
         return rc(cut(layer, p, to), landing(layer, p, t), *sems, (e, to))
 
@@ -348,7 +352,7 @@
             each(strips, strips + LAG, lambda c: mid_second(c - LAG))
 
     order = [(i, k) for i in range(n_outs) for k in range(TENSORS)]
-    offsets = range(1, TENSORS)
+    offsets = (2, 3, 1)
     z_plan = {}
     if first:
         for layer in range(2):
@@ -542,10 +546,10 @@
     place = lax.axis_index("tensor")
     sources = [staged]
     for k in range(TENSORS):
-        begin = (place + k) % TENSORS * q_width
+        begin = partner(place, k) * q_width
         piece = lax.dynamic_slice(last, (0, begin), (depth, q_width))
         if k > 0:
-            piece = lax.ppermute(piece, "tensor", [(i, (i + k) % TENSORS) for i in range(TENSORS)])
+            piece = lax.ppermute(piece, "tensor", [(i, partner(i, k)) for i in range(TENSORS)])
         sources.append(piece)
     for layer_number in range(layer_total):
         normed = norm_rows(residual, norm_gain[layer_number])

time: 497 us -> 491 us (0.988)
  Pallas kernels: 430 us -> 417 us
  starting transfers between devices: 21.1 us -> 27.8 us
    pallas_call x3, Pallas kernels: 414 us -> 402 us  [communicate(): pl.pallas_call(functools.partial(comm_kernel, parts, n, bool(sums)), out_...]
    ppermute x3, starting transfers between devices: 21.1 us -> 27.8 us  [fast_shards(): lax.ppermute(piece, 'tensor', [(i, partner(i, k)) for i in range(TENSORS)])]
where the time goes in v4:
time: 491 us; the launch traced here: 490 us
  Pallas kernels  417 us (85%)
  starting transfers between devices  27.8 us (6%)
  matrix products  24.5 us (5%)
  other arithmetic  10.1 us (2%)
  local copies, waits for them, and re-layouts  9.7 us (2%)
    pallas_call x3, Pallas kernels, communicate(): pl.pallas_call(functools.partial(comm_kernel, parts, n, bool(sums)), out_...  402 us
    ppermute x3, starting transfers between devices, fast_shards(): lax.ppermute(piece, 'tensor', [(i, partner(i, k)) for i in range(TENSORS)])  27.8 us
    dot_general x2, matrix products, fast_shards(): projected = jnp.dot(normed, qkv_weight, preferred_element_type=jnp.float32)  24.5 us
    pallas_call x2, Pallas kernels, attention(): pl.pallas_call(functools.partial(attention_kernel, heads, keys), out_shap...  15.9 us
  transfers between devices with their start and end apart: 3, of which 0 were waited for; matrix products, arithmetic and copies ran while one was open for 4% of the time, Pallas kernels for 2%

profile of v4, /device:TPU:0, one launch (start us, length us, event | category | flops | bytes accessed | tf_op | source)
XLA Modules:
  0.0 490.4 jit_solution(11881585692753595646)
XLA Ops:
  0.7 1.4 slice_bitcast_fusion
  2.1 0.0 copy-start.1
  2.1 1.3 copy-done.1
  3.4 126.9 %shard_map.95 = (bf16[8,4,160,1536]{3,2,1,0:T(8,128)(2,1)}, bf16[8,4,160,1024]{3,2,1,0:T(8,128)(2,1)}, bf16[4,160,1536]{2,1,0:T(8,128)(2,1)S(1)}) custom-call(bf16[2,160,4096]{2,1,0:T(8,128)(2,1)} %refs_0_.1, bf16[2,160,2048]{2,1,0:T(8,128)(2,1)S(1)} %copy-done.1, bf16[2,160,4096]{2,1,0:T(8,128)(2,1)} %bitcast.24), custom_call_target="tpu_custom_call" | custom-call | bytes 60000000 | tf_op jit(solution)/shard_map/pallas_call | solution.py:453
  130.3 0.0 copy-start
  130.3 1.3 copy-done
  131.5 0.0 copy-start.5
  131.5 0.0 copy-start.6
  131.5 0.0 copy-start.3
  131.5 0.1 constant_dynamic-slice_fusion
  131.7 1.6 collective-permute-start.2
  133.2 25.7 %collective-permute-start.1 = (bf16[160,1024]{1,0:T(8,128)(2,1)S(1)}, bf16[160,1024]{1,0:T(8,128)(2,1)S(1)}, u32[]{:S(2)}, u32[]{:S(2)}) collective-permute-start(bf16[160,1024]{1,0:T(8,128)(2,1)S(1)} %get-tuple-element.34), channel_id=1, source_target_pairs={{0,2},{1,3},{2,0},{3,1},{4,6},{5,7},{6,4},{7,5},{8,10},{9,11},{10,... | collective-permute-start | bytes 983048 | tf_op jit(solution)/shard_map/ppermute | solution.py:552
  159.0 0.5 collective-permute-start
  159.5 3.6 fusion
  163.1 0.0 copy-done.5
  163.1 0.0 copy-done.6
  163.1 0.1 copy.12
  163.2 0.1 reduce
  163.3 0.1 select_reduce_fusion
  163.4 0.0 copy-done.3
  163.5 0.2 fusion.15.allowed
  163.7 1.0 fusion.16
  164.7 0.0 copy-start.4
  164.7 13.1 %fusion.8.proj = f32[512,1536]{1,0:T(8,128)S(1)} fusion(bf16[5120,1536]{1,0:T(8,128)(2,1)} %bitcast.27, bf16[512,5120]{1,0:T(8,128)(2,1)} %refs_7_.1, f32[5120]{0:T(1024)S(1)} %bitcast.26, f32[512]{0:T(512)S(1)} %add_rsqrt_fusion.1), kind=kOutput, calls=%fused_computation.11 | convolution fusion | flops 8063549440 | bytes 24139776 | tf_op jit(solution)/shard_map/dot_general | solution.py:558
  177.8 0.2 pad_maximum_fusion.1
  178.0 0.0 copy-done.4
  178.0 8.0 %shard_map.96 = (bf16[512,1024]{1,0:T(8,128)(2,1)S(1)}, bf16[512,512]{1,0:T(8,128)(2,1)S(1)}) custom-call(f32[512,1536]{1,0:T(8,128)S(1)} %fusion.8.proj, f32[512,128]{1,0:T(8,128)S(1)} %get-tuple-element.44.cosine, f32[512,128]{1,0:T(8,128)S(1)} %get-tuple-element.45.sine_part, f32[2,128]{1,0:T(2,128)S(1)} %get-tuple-element.43.gain, ...), custom_call_target="tpu_custom_call" | custom-call | flops 1073741824 | bytes 6291456 | tf_op jit(solution)/shard_map/pallas_call | solution.py:508
  186.0 0.0 collective-permute-done.2.refs_4_
  186.0 0.0 collective-permute-done.1.refs_3_
  186.0 0.0 collective-permute-done.refs_2_
  186.0 141.8 %shard_map.97 = (bf16[8,4,160,1536]{3,2,1,0:T(8,128)(2,1)}, bf16[8,4,160,1024]{3,2,1,0:T(8,128)(2,1)}, bf16[512,5120]{1,0:T(8,128)(2,1)}) custom-call(bf16[4,160,1536]{2,1,0:T(8,128)(2,1)} %copy-done, bf16[160,1024]{1,0:T(8,128)(2,1)S(1)} %get-tuple-element.36.refs_1_, bf16[160,1024]{1,0:T(8,128)(2,1)S(1)} %collective-permute-done.refs_2_, ...), custom_call_target="tpu_custom_call" | custom-call | bytes 60000000 | tf_op jit(solution)/shard_map/pallas_call | solution.py:453
  327.9 0.0 copy-start.2
  327.9 3.7 fusion.3
  331.6 0.3 copy-done.2
  331.9 11.4 %fusion.6.proj = f32[512,1536]{1,0:T(8,128)S(1)} fusion(bf16[5120,1536]{1,0:T(8,128)(2,1)} %bitcast.28, bf16[512,5120]{1,0:T(8,128)(2,1)S(1)} %copy-done.2, f32[5120]{0:T(1024)S(1)} %bitcast.25, f32[512]{0:T(512)S(1)} %add_rsqrt_fusion), kind=kOutput, calls=%fused_computation.10 | convolution fusion | flops 8063549440 | bytes 24139776 | tf_op jit(solution)/shard_map/dot_general | solution.py:558
  343.3 8.0 %shard_map.98 = (bf16[512,1024]{1,0:T(8,128)(2,1)S(1)}, bf16[512,512]{1,0:T(8,128)(2,1)S(1)}) custom-call(f32[512,1536]{1,0:T(8,128)S(1)} %fusion.6.proj, f32[512,128]{1,0:T(8,128)S(1)} %get-tuple-element.44.cosine, f32[512,128]{1,0:T(8,128)S(1)} %get-tuple-element.45.sine_part, f32[2,128]{1,0:T(2,128)S(1)} %get-tuple-element.42.gain, ...), custom_call_target="tpu_custom_call" | custom-call | flops 1073741824 | bytes 6291456 | tf_op jit(solution)/shard_map/pallas_call | solution.py:508
  351.3 132.8 %shard_map.99 = bf16[512,5120]{1,0:T(8,128)(2,1)} custom-call(bf16[5120,1024]{1,0:T(8,128)(2,1)} %bitcast.22, bf16[512,1024]{1,0:T(8,128)(2,1)S(1)} %get-tuple-element.23.refs_1_, bf16[512,5120]{1,0:T(8,128)(2,1)} %get-tuple-element.21.refs_2_), custom_call_target="tpu_custom_call" | custom-call | bytes 60000000 | tf_op jit(solution)/shard_map/pallas_call | solution.py:453
  484.2 1.1 pad_maximum_fusion
  485.2 5.2 %copy.14 = bf16[512,5120]{1,0:T(8,128)(2,1)} copy(bf16[512,5120]{1,0:T(8,128)(2,1)} %shard_map.99) | data formatting | bytes 10485760
  (10 shorter events, 0.1 us)
Async XLA Ops:
  2.1 1.3 copy-start.1
  130.3 1.3 copy-start
  131.5 31.5 %copy-start.5 = (s32[16]{0:T(128)S(1)}, s32[16]{0:T(128)}, u32[]{:S(2)}) copy-start(s32[16]{0:T(128)} %param.9) | copy-start | bytes 196
  131.5 31.5 %copy-start.6 = (s32[16]{0:T(128)S(1)}, s32[16]{0:T(128)}, u32[]{:S(2)}) copy-start(s32[16]{0:T(128)} %param.10) | copy-start | bytes 196
  131.5 31.9 %copy-start.3 = (f32[2,5120]{1,0:T(2,128)S(1)}, f32[2,5120]{1,0:T(2,128)}, u32[]{:S(2)}) copy-start(f32[2,5120]{1,0:T(2,128)} %param.14) | copy-start | bytes 122884
  131.7 54.3 %collective-permute-start.2 = (bf16[160,1024]{1,0:T(8,128)(2,1)S(1)}, bf16[160,1024]{1,0:T(8,128)(2,1)S(1)}, u32[]{:S(2)}, u32[]{:S(2)}) collective-permute-start(bf16[160,1024]{1,0:T(8,128)(2,1)S(1)} %get-tuple-element.33), channel_id=1, source_target_pairs={{0,3},{1,2},{2,1},{3,0},{4,7},{5,6},{6,5},{7,4},{8,11},{9,10},{10,... | collective-permute-start | bytes 983048 | tf_op jit(solution)/shard_map/ppermute | solution.py:552
  133.2 52.8 %collective-permute-start.1 = (bf16[160,1024]{1,0:T(8,128)(2,1)S(1)}, bf16[160,1024]{1,0:T(8,128)(2,1)S(1)}, u32[]{:S(2)}, u32[]{:S(2)}) collective-permute-start(bf16[160,1024]{1,0:T(8,128)(2,1)S(1)} %get-tuple-element.34), channel_id=1, source_target_pairs={{0,2},{1,3},{2,0},{3,1},{4,6},{5,7},{6,4},{7,5},{8,10},{9,11},{10,... | collective-permute-start | bytes 983048 | tf_op jit(solution)/shard_map/ppermute | solution.py:552
  159.0 27.1 %collective-permute-start = (bf16[160,1024]{1,0:T(8,128)(2,1)S(1)}, bf16[160,1024]{1,0:T(8,128)(2,1)S(1)}, u32[]{:S(2)}, u32[]{:S(2)}) collective-permute-start(bf16[160,1024]{1,0:T(8,128)(2,1)S(1)} %get-tuple-element.35), channel_id=1, source_target_pairs={{0,1},{1,0},{2,3},{3,2},{4,5},{5,4},{6,7},{7,6},{8,9},{9,8},{10,11... | collective-permute-start | bytes 983048 | tf_op jit(solution)/shard_map/ppermute | solution.py:552
  164.7 13.3 %copy-start.4 = (f32[2,2,128]{2,1,0:T(2,128)S(1)}, f32[2,2,128]{2,1,0:T(2,128)}, u32[]{:S(2)}) copy-start(f32[2,2,128]{2,1,0:T(2,128)} %param.15) | copy-start | bytes 6148
  327.9 4.0 copy-start.2
